TPU v7x, 32 devices: a whole 2x2x4 slice. The times are simulated.
32 devices in a mesh: inp: 2 (over x), tm: 16 (over z, y, core).
Axes of the slice: x: 2, y: 2, z: 4, core: 2. Of those that a mesh axis runs over, the one named last changes fastest.
Arguments:
- raw: bfloat16 [1024, 131072], P('inp', 'tm'), may hold values from -6 to 6
- taps: float32 [4, 512], replicated, may hold values from -3 to 3
Outputs:
- visibilities: float32 [256, 2, 1024, 1024], P('tm', None, 'inp')
All inputs are finite; a program needn't handle non-finite values.
Results may differ from a plain program's by a relative error of at most 0.0052.
Values may be sent and summed in bfloat16 or wider, within the bound.
No kernel may reach another device: no remote copies, remote signals or barrier semaphores. Data moves between devices by JAX's collectives and lax.ppermute only.
A program may use at most 256 MiB of HBM per device.

v0:
```python
import math

import jax
import jax.numpy as jnp
from jax import lax
from jax.sharding import PartitionSpec as P


def from_behind(value, axis, by):
    devices = lax.axis_size(axis)
    pairs = [(i, i + by) for i in range(devices) if 0 <= i + by < devices]
    return lax.ppermute(value, axis, pairs)


def from_partner(value, axis, stride):
    return lax.ppermute(value, axis, [(i, i ^ 1 << stride) for i in range(lax.axis_size(axis))])


def dft_table(length):
    half = length // 2
    kidx = jnp.arange(half, dtype=jnp.int32)[:, None]
    nidx = jnp.arange(length, dtype=jnp.int32)[None, :]
    phase = (kidx * nidx % length).astype(jnp.float32) * (2.0 * math.pi / length)
    norm = 1.0 / math.sqrt(length)
    return jnp.stack([jnp.cos(phase) * norm, -jnp.sin(phase) * norm], axis=1).astype(jnp.bfloat16)


def cross_power(rows, cols, count):
    rotated = jnp.stack([cols[:, 1], -cols[:, 0]], axis=1)
    real_part = jnp.einsum("crsi,crsj->cij", rows, cols, preferred_element_type=jnp.float32)
    imag_part = jnp.einsum("crsi,crsj->cij", rows, rotated, preferred_element_type=jnp.float32)
    return jnp.stack([real_part, imag_part], axis=1) / count


def per_device(raw, taps):
    n_taps, length = taps.shape
    block_inputs, local_samples = raw.shape
    spec_local = local_samples // length
    frames = raw.reshape(block_inputs, spec_local, length)
    tail = frames[:, spec_local - (n_taps - 1) :, :]
    before = from_behind(tail, "tm", 1)
    extended = jnp.concatenate([before, frames], axis=1)
    filtered = sum(
        (taps[t][None, None, :] * extended[:, t : t + spec_local, :] for t in range(n_taps))
    )
    filtered = filtered.astype(jnp.bfloat16)
    table = dft_table(length)
    spectra = jnp.einsum(
        "isn,crn->crsi", filtered, table, preferred_element_type=jnp.float32
    ).astype(jnp.bfloat16)
    turned = lax.all_to_all(spectra, "tm", split_axis=0, concat_axis=2, tiled=True)
    count = turned.shape[2]
    group = lax.axis_index("inp")
    first = group == 0
    other = from_partner(turned, "inp", 0)
    leading = jnp.where(first, turned, other)
    trailing = jnp.where(first, other, turned)
    columns = jnp.concatenate([leading, trailing], axis=3)
    return cross_power(turned, columns, count)


def solution(mesh):
    return jax.shard_map(
        per_device,
        mesh=mesh,
        in_specs=(P("inp", "tm"), P()),
        out_specs=P("tm", None, "inp", None),
        check_vma=False,
    )
```

profile of v0, /device:TPU:0, one launch (start us, length us, event | category | flops | bytes accessed | tf_op | source)
XLA Modules:
  0.0 604.1 jit_solution(6823504216060345752)
XLA Ops:
  0.0 0.0 copy-start.2
  0.0 7.7 %copy.30 = bf16[64,16,8,512]{3,2,0,1:T(8,128)(2,1)} copy(bf16[64,16,8,512]{3,2,1,0:T(8,128)(2,1)} %bitcast.44) | data formatting | bytes 16777216 | tf_op jit(solution)/shard_map/reshape | solution.py:39
  7.7 1.5 slice.40
  9.2 2.5 collective-permute-start
  11.7 2.2 multiply_convert_fusion
  13.9 0.0 copy-done.2
  13.9 0.7 collective-permute-done
  14.6 1.2 constant_dynamic-update-slice_fusion.1
  15.8 7.7 %constant_dynamic-update-slice_fusion = bf16[512,19,512]{2,0,1:T(8,128)(2,1)} fusion(bf16[512,19,512]{2,0,1:T(8,128)(2,1)} %constant_dynamic-update-slice_fusion.1, bf16[64,16,8,512]{3,2,1,0:T(8,128)(2,1)} %bitcast.45), kind=kLoop, calls=%fused_computation.42 | loop fusion | bytes 16777216 | tf_op jit(solution)/shard_map/concatenate | solution.py:42
  23.5 16.6 %convert_bitcast_fusion = bf16[256,2,16,512]{3,0,2,1:T(8,128)(2,1)} fusion(bf16[512,19,512]{2,0,1:T(8,128)(2,1)} %constant_dynamic-update-slice_fusion, f32[512]{0:T(512)S(1)} %bitcast.51, f32[512]{0:T(512)S(1)} %bitcast.52, f32[512]{0:T(512)S(1)} %bitcast.50, f32[512]{0:T(512)S(1)} %bitcast.49, bf16[256,1,512]{2,0,1:T(8,128)(2,1)S(1)} %get-tuple-element.13, ...), kind=kOutput, calls=%fused_computation.21 | convolution fusion | flops 4350541824 | bytes 42475520 | tf_op jit(solution)/shard_map/isn,crn->crsi/dot_general | solution.py:48
  40.1 11.5 %copy.13 = bf16[256,2,16,512]{3,2,1,0:T(8,128)(2,1)} copy(bf16[256,2,16,512]{3,0,2,1:T(8,128)(2,1)} %convert_bitcast_fusion) | data formatting | bytes 16777216 | tf_op jit(solution)/shard_map/convert_element_type | solution.py:50
  51.6 206.0 %all_to_all.18 = bf16[256,2,16,512]{3,2,1,0:T(8,128)(2,1)} all-to-all(bf16[256,2,16,512]{3,2,1,0:T(8,128)(2,1)} %copy.13), channel_id=1, replica_groups=mesh['inp'=2,'tm'=16] {'tm'}, dimensions={0} | all-to-all | bytes 16777216 | tf_op jit(solution)/shard_map/all_to_all | solution.py:51
  257.6 8.1 %copy.14 = bf16[16,16,2,16,512]{4,3,0,2,1:T(8,128)(2,1)} copy(bf16[16,16,2,16,512]{4,3,2,1,0:T(8,128)(2,1)} %bitcast.47) | data formatting | bytes 16777216 | tf_op jit(solution)/shard_map/all_to_all | solution.py:51
  265.7 1.5 collective-permute-start.1
  267.2 182.0 %collective-permute-done.1 = bf16[16,2,256,512]{3,2,1,0:T(8,128)(2,1)} collective-permute-done((bf16[16,2,256,512]{3,2,1,0:T(8,128)(2,1)}, bf16[16,2,256,512]{3,2,1,0:T(8,128)(2,1)}, u32[]{:S(2)}, u32[]{:S(2)}) %collective-permute-start.1) | collective-permute-done | bytes 8388640 | tf_op jit(solution)/shard_map/ppermute | solution.py:16
  449.1 6.5 %broadcast_select_fusion = (bf16[16,2,256,512]{3,2,1,0:T(8,128)(2,1)S(1)}, bf16[16,2,256,512]{3,2,1,0:T(8,128)(2,1)S(1)}) fusion(bf16[16,2,256,512]{3,2,1,0:T(8,128)(2,1)} %collective-permute-done.1, pred[]{:T(512)S(6)} %eq.5, bf16[16,16,2,16,512]{4,3,0,2,1:T(8,128)(2,1)} %copy.14), kind=kLoop, calls=%fused_computation.26 | loop fusion | flops 8388608 | bytes 33554432 | tf_op jit(solution)/shard_map/jit(_where)/select_n | solution.py:57
  455.6 0.0 copy-start
  455.6 0.0 copy-start.1
  455.6 3.4 copy-done
  459.0 2.6 copy-done.1
  461.6 7.0 %fusion.10 = (bf16[16,1,256,1024]{3,2,1,0:T(8,128)(2,1)}, bf16[16,1,256,1024]{3,2,1,0:T(8,128)(2,1)}) fusion(bf16[16,2,256,512]{3,2,1,0:T(8,128)(2,1)S(1)} %get-tuple-element.8, bf16[16,2,256,512]{3,2,1,0:T(8,128)(2,1)S(1)} %get-tuple-element.7), kind=kLoop, calls=%fused_computation.15 | loop fusion | flops 37748736 | bytes 33554432 | tf_op jit(solution)/shard_map/concatenate | solution.py:58
  468.6 24.3 %fusion.8 = f32[16,1,512,1024]{3,2,0,1:T(8,128)} fusion(bf16[16,2,256,512]{3,2,1,0:T(8,128)(2,1)} %bitcast.42, bf16[16,2,256,512]{3,2,1,0:T(8,128)(2,1)} %copy-done, bf16[16,2,256,512]{3,2,1,0:T(8,128)(2,1)} %copy-done.1), kind=kOutput, calls=%fused_computation.13 | convolution fusion | flops 8623489024 | bytes 58720256 | tf_op jit(solution)/shard_map/crsi,crsj->cij/dot_general | solution.py:30
  492.9 23.0 %fusion.5 = f32[16,1,512,1024]{3,2,0,1:T(8,128)} fusion(bf16[16,2,256,512]{3,2,1,0:T(8,128)(2,1)} %bitcast.43, bf16[16,1,256,1024]{3,2,1,0:T(8,128)(2,1)} %get-tuple-element.6, bf16[16,1,256,1024]{3,2,1,0:T(8,128)(2,1)} %get-tuple-element.5), kind=kOutput, calls=%fused_computation.12 | convolution fusion | flops 8598323200 | bytes 58720256 | tf_op jit(solution)/shard_map/crsi,crsj->cij/dot_general | solution.py:31
  515.9 44.5 %maximum_multiply_fusion = f32[16,2,512,1024]{3,2,0,1:T(8,128)} fusion(f32[16,1,512,1024]{3,2,0,1:T(8,128)} %fusion.5, f32[16,1,512,1024]{3,2,0,1:T(8,128)} %fusion.8), kind=kLoop, calls=%fused_computation | loop fusion | flops 33554432 | bytes 134217728 | tf_op jit(solution)/shard_map/div | solution.py:32
  560.4 43.8 %copy.17 = f32[16,2,512,1024]{3,2,1,0:T(8,128)} copy(f32[16,2,512,1024]{3,2,0,1:T(8,128)} %maximum_multiply_fusion) | data formatting | bytes 134217728 | tf_op jit(solution)/shard_map/div | solution.py:32
  (1 shorter events, 0.0 us)
Async XLA Ops:
  0.0 13.9 %copy-start.2 = (f32[4,512]{1,0:T(4,128)S(1)}, f32[4,512]{1,0:T(4,128)}, u32[]{:S(2)}) copy-start(f32[4,512]{1,0:T(4,128)} %param.3) | copy-start | bytes 24580
  9.2 5.4 collective-permute-start
  265.7 183.4 %collective-permute-start.1 = (bf16[16,2,256,512]{3,2,1,0:T(8,128)(2,1)}, bf16[16,2,256,512]{3,2,1,0:T(8,128)(2,1)}, u32[]{:S(2)}, u32[]{:S(2)}) collective-permute-start(bf16[16,2,256,512]{3,2,1,0:T(8,128)(2,1)} %bitcast.41), channel_id=1, source_target_pairs={{0,16},{16,0},{1,17},{17,1},{2,18},{18,2},{3,19},{19,3},{4,20},{20... | collective-permute-start | bytes 25165832 | tf_op jit(solution)/shard_map/ppermute | solution.py:16
  455.6 3.4 copy-start
  455.6 6.0 copy-start.1
where the time goes:
time: 604 us
  blocking collectives  206 us (34%)
  waiting for transfers between devices  183 us (30%)
  local copies, waits for them, and re-layouts  87.4 us (14%)
  matrix products  63.9 us (11%)
  other arithmetic  60.1 us (10%)
    all_to_all x1, blocking collectives, per_device(): lax.all_to_all(spectra, 'tm', split_axis=0, concat_axis=2, tiled=True)  206 us
    ppermute x1, waiting for transfers between devices, from_partner(): lax.ppermute(value, axis, [(i, i ^ 1 << stride) for i in range(lax.axis_s...  182 us
    div x1, other arithmetic, cross_power(): return jnp.stack([real_part, imag_part], axis=1) / count  44.5 us
    div x1, local copies, waits for them, and re-layouts, cross_power(): return jnp.stack([real_part, imag_part], axis=1) / count  43.8 us
    dot_general x1, matrix products, cross_power(): jnp.einsum('crsi,crsj->cij', rows, cols, preferred_element_type=jnp.float32)  24.3 us
    dot_general x1, matrix products, cross_power(): jnp.einsum('crsi,crsj->cij', rows, rotated, preferred_element_type=jnp.fl...  23 us
    dot_general x1, matrix products, per_device(): jnp.einsum('isn,crn->crsi', filtered, table, preferred_element_type=jnp.f...  16.6 us
  transfers between devices with their start and end apart: 2, of which 2 were waited for; matrix products, arithmetic and copies ran while one was open for 0% of the time, Pallas kernels for 0%

commit v1 on v0

v1 whole, which is shorter than its diff:
```python
import functools
import math

import jax
import jax.numpy as jnp
import numpy as np
from jax import lax
from jax.experimental import pallas as pl
from jax.experimental.pallas import tpu as pltpu
from jax.sharding import PartitionSpec as P

VMEM_LIMIT = 56 << 20


def after(value, earlier):
    return lax.optimization_barrier((value, *earlier))[0] if earlier else value


def from_behind(value, axis):
    devices = lax.axis_size(axis)
    return lax.ppermute(value, axis, [(i, i + 1) for i in range(devices - 1)])


def from_partner(value, axis):
    return lax.ppermute(value, axis, [(i, i ^ 1) for i in range(lax.axis_size(axis))])


def part_sizes(channels):
    part = max(1, channels // 4)
    return [part] * (channels // part) + [1] * (channels % part)


def dft_rows(length, devices, sizes):
    channels = length // 2
    own = channels // devices
    order = []
    first = 0
    for size in sizes:
        for owner in range(devices):
            order += range(owner * own + first, owner * own + first + size)
        first += size
    k = np.asarray(order)[:, None]
    phase = (k * np.arange(length)[None, :] % length) * (2.0 * math.pi / length)
    norm = 1.0 / math.sqrt(length)
    table = np.stack([np.cos(phase) * norm, -np.sin(phase) * norm], axis=1)
    return jnp.asarray(table.reshape(2 * channels, length), jnp.bfloat16)


def spectra_body(frames, length, group, taps_ref, table_ref, order_ref, raw_ref, halo_ref, *refs):
    *outs, scratch = refs
    n_taps = taps_ref.shape[0]
    taps = taps_ref[...]
    table = table_ref[...]

    def frame(f):
        ref, at = (halo_ref, f) if f < n_taps - 1 else (raw_ref, f - (n_taps - 1))
        return ref[:, at * length : (at + 1) * length].astype(jnp.float32)

    for s in range(frames):
        total = taps[0:1] * frame(s)
        for t in range(1, n_taps):
            total = total + taps[t : t + 1] * frame(s + t)
        spectrum = lax.dot_general(
            table,
            total.astype(jnp.bfloat16),
            (((1,), (1,)), ((), ())),
            preferred_element_type=jnp.float32,
        )
        scratch[s] = spectrum.astype(jnp.bfloat16)
    first = 0
    width = raw_ref.shape[0]
    for out in outs:
        for at in range(0, out.shape[0], group):
            mixed = scratch[:, first + at : first + at + group, :].reshape(group * frames, width)
            rows = jnp.dot(order_ref[...], mixed, preferred_element_type=jnp.float32)
            out[at : at + group] = rows.astype(jnp.bfloat16).reshape(group, frames, width)
        first += out.shape[0]


def make_spectra(raw, halo, taps, devices, sizes):
    n_taps, length = taps.shape
    inputs, samples = raw.shape
    frames = samples // length
    rows = length
    block = min(inputs, 256)
    group = 16
    order = np.zeros((group, frames, frames, group), np.float32)
    for r in range(group):
        for s in range(frames):
            order[r, s, s, r] = 1.0
    order = jnp.asarray(order.reshape(group * frames, group * frames), jnp.bfloat16)
    table = dft_rows(length, devices, sizes)
    counts = [devices * size * 2 for size in sizes]
    outs = pl.pallas_call(
        functools.partial(spectra_body, frames, length, group),
        grid=(inputs // block,),
        in_specs=[
            pl.BlockSpec(taps.shape, lambda i: (0, 0)),
            pl.BlockSpec(table.shape, lambda i: (0, 0)),
            pl.BlockSpec(order.shape, lambda i: (0, 0)),
            pl.BlockSpec((block, samples), lambda i: (i, 0)),
            pl.BlockSpec((block, halo.shape[1]), lambda i: (i, 0)),
        ],
        out_specs=[pl.BlockSpec((c, frames, block), lambda i: (0, 0, i)) for c in counts],
        out_shape=[jax.ShapeDtypeStruct((c, frames, inputs), jnp.bfloat16) for c in counts],
        scratch_shapes=[pltpu.VMEM((frames, rows, block), jnp.bfloat16)],
        compiler_params=pltpu.CompilerParams(vmem_limit_bytes=VMEM_LIMIT),
        cost_estimate=pl.CostEstimate(
            flops=2 * inputs * frames * rows * length,
            bytes_accessed=4 * inputs * samples,
            transcendentals=0,
        ),
        name="spectra",
    )(taps, table, order, raw, halo)
    return [
        out.reshape(devices, size, 2, frames, inputs) for out, size in zip(outs, sizes)
    ]


def correlate_body(count, group_ref, own_ref, other_ref, *refs):
    out_ref = refs[-1]
    sources, _, _, frames, inputs = own_ref.shape
    depth = sources * frames

    def parts(ref):
        return ref[:, 0, 0].reshape(depth, inputs), ref[:, 0, 1].reshape(depth, inputs)

    own = parts(own_ref)
    other = parts(other_ref)
    rows = jnp.transpose(jnp.concatenate(own, axis=0))

    def store(column, real, imag):
        where = slice(column, column + inputs)
        for which, pair in enumerate(((real, imag), (imag, -real))):
            product = jnp.dot(
                rows, jnp.concatenate(pair, axis=0), preferred_element_type=jnp.float32
            )
            out_ref[0, which, :, where] = product * (1.0 / count)

    @pl.when(group_ref[0] == 0)
    def _():
        store(0, *own)
        store(inputs, *other)

    @pl.when(group_ref[0] != 0)
    def _():
        store(inputs, *own)
        store(0, *other)


def correlate(group, own, other, earlier, shape, first, count):
    sources, channels, _, frames, inputs = own.shape
    held = [] if earlier is None else [earlier]
    spec = pl.BlockSpec((sources, 1, 2, frames, inputs), lambda c, g: (0, c, 0, 0, 0))
    return pl.pallas_call(
        functools.partial(correlate_body, count),
        grid_spec=pltpu.PrefetchScalarGridSpec(
            num_scalar_prefetch=1,
            grid=(channels,),
            in_specs=[spec, spec] + [pl.BlockSpec(memory_space=pl.ANY)] * len(held),
            out_specs=pl.BlockSpec(
                (1, 2, inputs, shape[3]), lambda c, g: (first + c, 0, 0, 0)
            ),
        ),
        out_shape=jax.ShapeDtypeStruct(shape, jnp.float32),
        input_output_aliases={3: 0} if held else {},
        compiler_params=pltpu.CompilerParams(vmem_limit_bytes=VMEM_LIMIT),
        cost_estimate=pl.CostEstimate(
            flops=channels * 16 * inputs * inputs * sources * frames,
            bytes_accessed=channels * 4 * inputs * (4 * inputs + 2 * sources * frames),
            transcendentals=0,
        ),
        name="correlate",
    )(group, own, other, *held)


def per_device(raw, taps):
    n_taps, length = taps.shape
    inputs, samples = raw.shape
    devices = lax.axis_size("tm")
    own_channels = length // 2 // devices
    count = samples // length * devices
    sizes = part_sizes(own_channels)
    halo = from_behind(raw[:, samples - (n_taps - 1) * length :], "tm")
    spectra = make_spectra(raw, halo, taps, devices, sizes)
    group = lax.axis_index("inp")[None]
    shape = (own_channels, 2, inputs, inputs * lax.axis_size("inp"))
    result = None
    turned, others = [], []
    for u, part in enumerate(spectra):
        part = after(part, others[u - 2 : u - 1] if u >= 2 else [])
        turned.append(lax.all_to_all(part, "tm", split_axis=0, concat_axis=0, tiled=True))
        others.append(from_partner(turned[u], "inp"))
    first = 0
    for size, own, other in zip(sizes, turned, others):
        result = correlate(group, own, other, result, shape, first, count)
        first += size
    return result


def solution(mesh):
    return jax.shard_map(
        per_device,
        mesh=mesh,
        in_specs=(P("inp", "tm"), P()),
        out_specs=P("tm", None, "inp", None),
        check_vma=False,
    )
```

time: 604 us -> 314 us (0.52)
  blocking collectives: 206 us -> 71.2 us
  local copies, waits for them, and re-layouts: 87.4 us -> 5.38 us
  matrix products: 63.9 us -> 0 us
  other arithmetic: 60.1 us -> 0 us
  Pallas kernels: 0 us -> 54.2 us
  waiting for transfers between devices: 183 us -> 156 us
  starting transfers between devices: 3.94 us -> 25.3 us
    all_to_all x1, blocking collectives: 206 us -> 71.2 us  [per_device(): lax.all_to_all(part, 'tm', split_axis=0, concat_axis=0, tiled=True)]
    ppermute x2 -> x5, waiting for transfers between devices: 183 us -> 116 us  [the longest x4 113 us: from_partner(): lax.ppermute(value, axis, [(i, i ^ 1) for i in range(lax.axis_size(axis))])]
    dot_general x3 -> x0, matrix products: 63.9 us -> none  [the longest x1 24.3 us: cross_power(): jnp.einsum('crsi,crsj->cij', rows, cols, preferred_element_type=jnp.float32)]
    pallas_call x0 -> x5, Pallas kernels: none -> 54.2 us  [the longest x4 40.6 us: correlate(): pl.pallas_call(functools.partial(correlate_body, count), grid_spec=pltpu....]
    div x1 -> x0, other arithmetic: 44.5 us -> none  [cross_power(): return jnp.stack([real_part, imag_part], axis=1) / count]
    div x1 -> x0, local copies, waits for them, and re-layouts: 43.8 us -> none  [cross_power(): return jnp.stack([real_part, imag_part], axis=1) / count]
    all_to_all x0 -> x3, waiting for transfers between devices: none -> 39.5 us  [per_device(): lax.all_to_all(part, 'tm', split_axis=0, concat_axis=0, tiled=True)]
    all_to_all x0 -> x3, starting transfers between devices: none -> 16.7 us  [per_device(): lax.all_to_all(part, 'tm', split_axis=0, concat_axis=0, tiled=True)]
  transfers between devices with their start and end apart: 2 -> 8, of which waited for: 2 -> 5; matrix products, arithmetic and copies ran while one was open for 0% -> 0% of each run, Pallas kernels for 0% -> 10%
where the time goes in v1:
time: 314 us; the launch traced here: 312 us
  waiting for transfers between devices  156 us (50%)
  blocking collectives  71.2 us (23%)
  Pallas kernels  54.2 us (17%)
  starting transfers between devices  25.3 us (8%)
  local copies, waits for them, and re-layouts  5.38 us (2%)
    ppermute x4, waiting for transfers between devices, from_partner(): lax.ppermute(value, axis, [(i, i ^ 1) for i in range(lax.axis_size(axis))])  113 us
    all_to_all x1, blocking collectives, per_device(): lax.all_to_all(part, 'tm', split_axis=0, concat_axis=0, tiled=True)  71.2 us
    pallas_call x4, Pallas kernels, correlate(): pl.pallas_call(functools.partial(correlate_body, count), grid_spec=pltpu....  40.6 us
    all_to_all x3, waiting for transfers between devices, per_device(): lax.all_to_all(part, 'tm', split_axis=0, concat_axis=0, tiled=True)  39.5 us
    all_to_all x3, starting transfers between devices, per_device(): lax.all_to_all(part, 'tm', split_axis=0, concat_axis=0, tiled=True)  16.7 us
    pallas_call x1, Pallas kernels, make_spectra(): pl.pallas_call(functools.partial(spectra_body, frames, length, group), gr...  13.7 us
  transfers between devices with their start and end apart: 8, of which 5 were waited for; matrix products, arithmetic and copies ran while one was open for 0% of the time, Pallas kernels for 10%

profile of v1, /device:TPU:0, one launch (start us, length us, event | category | flops | bytes accessed | tf_op | source)
XLA Modules:
  0.0 311.8 jit_solution(9957539727168174432)
XLA Ops:
  0.0 1.5 slice.3
  1.5 2.5 collective-permute-start
  4.0 2.9 collective-permute-done.halo_ref
  6.9 0.0 copy-start.4
  6.9 1.2 copy-done.4
  8.1 13.7 %spectra.1 = (bf16[128,16,512]{2,1,0:T(8,128)(2,1)}, bf16[128,16,512]{2,1,0:T(8,128)(2,1)}, bf16[128,16,512]{2,1,0:T(8,128)(2,1)}, bf16[128,16,512]{2,1,0:T(8,128)(2,1)}) custom-call(f32[4,512]{1,0:T(4,128)} %taps_ref.1, bf16[512,512]{1,0:T(8,128)(2,1)} %constant.11.clone.table_ref, bf16[256,256]{1,0:T(8,128)(2,1)} %constant.10.clone.order_ref, ...), custom_call_target="tpu_custom_call" | custom-call | flops 4294967296 | bytes 16777216 | tf_op jit(solution)/shard_map/spectra/pallas_call | solution.py:94
  21.7 71.2 %all_to_all.20.own_ref = bf16[16,4,2,16,512]{4,3,2,1,0:T(8,128)(2,1)} all-to-all(bf16[16,4,2,16,512]{4,3,2,1,0:T(8,128)(2,1)} %bitcast.8), channel_id=1, replica_groups=mesh['inp'=2,'tm'=16] {'tm'}, dimensions={0} | all-to-all | bytes 4194304 | tf_op jit(solution)/shard_map/all_to_all | solution.py:192
  92.9 5.1 %all-to-all-start = ((bf16[16,4,2,16,512]{4,3,2,1,0:T(8,128)(2,1)}), bf16[16,4,2,16,512]{4,3,2,1,0:T(8,128)(2,1)S(1)}, u32[]{:S(2)}, u32[]{:S(2)}) async-start(bf16[16,4,2,16,512]{4,3,2,1,0:T(8,128)(2,1)} %bitcast.7), calls=%async_computation | async-start | bytes 4194304 | tf_op jit(solution)/shard_map/all_to_all | solution.py:192
  98.0 1.6 collective-permute-start.3
  99.6 46.6 %collective-permute-done.3.other_ref = bf16[16,4,2,16,512]{4,3,2,1,0:T(8,128)(2,1)S(1)} collective-permute-done((bf16[16,4,2,16,512]{4,3,2,1,0:T(8,128)(2,1)}, bf16[16,4,2,16,512]{4,3,2,1,0:T(8,128)(2,1)S(1)}, u32[]{:S(2)}, u32[]{:S(2)}) %collective-permute-start.3) | collective-permute-done | bytes 2097184 | tf_op jit(solution)/shard_map/ppermute | solution.py:25
  146.2 0.0 copy-start.3
  146.2 1.4 copy-done.3
  147.5 0.0 all-to-all-done.own_ref
  147.5 0.0 copy-start
  147.5 5.8 %all-to-all-start.3 = ((bf16[16,4,2,16,512]{4,3,2,1,0:T(8,128)(2,1)}), bf16[16,4,2,16,512]{4,3,2,1,0:T(8,128)(2,1)}, u32[]{:S(2)}, u32[]{:S(2)}) async-start(bf16[16,4,2,16,512]{4,3,2,1,0:T(8,128)(2,1)} %bitcast.6), calls=%async_computation.3 | async-start | bytes 4194304 | tf_op jit(solution)/shard_map/all_to_all | solution.py:192
  153.3 0.0 copy-done
  153.3 1.6 collective-permute-start.1
  154.9 46.4 %collective-permute-done.1.other_ref = bf16[16,4,2,16,512]{4,3,2,1,0:T(8,128)(2,1)S(1)} collective-permute-done((bf16[16,4,2,16,512]{4,3,2,1,0:T(8,128)(2,1)S(1)}, bf16[16,4,2,16,512]{4,3,2,1,0:T(8,128)(2,1)S(1)}, u32[]{:S(2)}, u32[]{:S(2)}) %collective-permute-start.1) | collective-permute-done | bytes 2097184 | tf_op jit(solution)/shard_map/ppermute | solution.py:25
  201.3 0.0 copy-start.2
  201.3 1.3 copy-done.2
  202.6 0.0 all-to-all-done.3.own_ref
  202.6 5.8 %all-to-all-start.1 = ((bf16[16,4,2,16,512]{4,3,2,1,0:T(8,128)(2,1)}), bf16[16,4,2,16,512]{4,3,2,1,0:T(8,128)(2,1)S(1)}, u32[]{:S(2)}, u32[]{:S(2)}) async-start(bf16[16,4,2,16,512]{4,3,2,1,0:T(8,128)(2,1)} %bitcast.5), calls=%async_computation.1 | async-start | bytes 4194304 | tf_op jit(solution)/shard_map/all_to_all | solution.py:192
  208.4 1.6 collective-permute-start.4
  210.0 39.5 %all-to-all-done.1.own_ref = bf16[16,4,2,16,512]{4,3,2,1,0:T(8,128)(2,1)S(1)} async-done(((bf16[16,4,2,16,512]{4,3,2,1,0:T(8,128)(2,1)}), bf16[16,4,2,16,512]{4,3,2,1,0:T(8,128)(2,1)S(1)}, u32[]{:S(2)}, u32[]{:S(2)}) %all-to-all-start.1) | async-done | bytes 2097184 | tf_op jit(solution)/shard_map/all_to_all | solution.py:192
  249.5 0.0 copy-start.1
  249.5 1.5 collective-permute-start.2
  251.0 10.1 %correlate.4.refs_0_ = f32[16,2,512,1024]{3,2,1,0:T(8,128)} custom-call(s32[1]{0:T(128)} %bitcast.group_ref, bf16[16,4,2,16,512]{4,3,2,1,0:T(8,128)(2,1)} %all_to_all.20.own_ref, bf16[16,4,2,16,512]{4,3,2,1,0:T(8,128)(2,1)} %copy-done.3), custom_call_target="tpu_custom_call" | custom-call | flops 4294967296 | bytes 20971520 | tf_op jit(solution)/shard_map/correlate/pallas_call | solution.py:155
  261.2 0.0 copy-done.1
  261.2 10.1 %correlate.5.refs_0_ = f32[16,2,512,1024]{3,2,1,0:T(8,128)} custom-call(s32[1]{0:T(128)} %bitcast.group_ref, bf16[16,4,2,16,512]{4,3,2,1,0:T(8,128)(2,1)} %copy-done, bf16[16,4,2,16,512]{4,3,2,1,0:T(8,128)(2,1)} %copy-done.2, f32[16,2,512,1024]{3,2,1,0:T(8,128)} %correlate.4.refs_0_), custom_call_target="tpu_custom_call", output_to_operand_aliasing={{}: (3, {})} | custom-call | flops 4294967296 | bytes 20971520 | tf_op jit(solution)/shard_map/correlate/pallas_call | solution.py:155
  271.3 0.0 collective-permute-done.4.other_ref
  271.3 10.1 %correlate.6.refs_0_ = f32[16,2,512,1024]{3,2,1,0:T(8,128)} custom-call(s32[1]{0:T(128)} %bitcast.group_ref, bf16[16,4,2,16,512]{4,3,2,1,0:T(8,128)(2,1)} %all-to-all-done.3.own_ref, bf16[16,4,2,16,512]{4,3,2,1,0:T(8,128)(2,1)} %collective-permute-done.4.other_ref, f32[16,2,512,1024]{3,2,1,0:T(8,128)} %correlate.5.refs_0_), custom_call_target="tpu_custom_call", output_to_operand_aliasing={{}: (3, {})} | custom-call | flops 4294967296 | bytes 20971520 | tf_op jit(solution)/shard_map/correlate/pallas_call | solution.py:155
  281.4 20.2 %collective-permute-done.2.other_ref = bf16[16,4,2,16,512]{4,3,2,1,0:T(8,128)(2,1)} collective-permute-done((bf16[16,4,2,16,512]{4,3,2,1,0:T(8,128)(2,1)S(1)}, bf16[16,4,2,16,512]{4,3,2,1,0:T(8,128)(2,1)}, u32[]{:S(2)}, u32[]{:S(2)}) %collective-permute-start.2) | collective-permute-done | bytes 2097184 | tf_op jit(solution)/shard_map/ppermute | solution.py:25
  301.7 10.1 %correlate.7 = f32[16,2,512,1024]{3,2,1,0:T(8,128)} custom-call(s32[1]{0:T(128)} %bitcast.group_ref, bf16[16,4,2,16,512]{4,3,2,1,0:T(8,128)(2,1)} %copy-done.1, bf16[16,4,2,16,512]{4,3,2,1,0:T(8,128)(2,1)} %collective-permute-done.2.other_ref, f32[16,2,512,1024]{3,2,1,0:T(8,128)} %correlate.6.refs_0_), custom_call_target="tpu_custom_call", output_to_operand_aliasing={{}: (3, {})} | custom-call | flops 4294967296 | bytes 20971520 | tf_op jit(solution)/shard_map/correlate/pallas_call | solution.py:155
Async XLA Ops:
  1.5 5.4 %collective-permute-start = (bf16[512,1536]{1,0:T(8,128)(2,1)S(1)}, bf16[512,1536]{1,0:T(8,128)(2,1)S(1)}, u32[]{:S(2)}, u32[]{:S(2)}) collective-permute-start(bf16[512,1536]{1,0:T(8,128)(2,1)S(1)} %slice.3), channel_id=1, source_target_pairs={{0,1},{1,2},{2,3},{3,4},{4,5},{5,6},{6,7},{7,8},{8,9},{9,10},{10,1... | collective-permute-start | bytes 4718600 | tf_op jit(solution)/shard_map/ppermute | solution.py:21
  6.9 1.2 copy-start.4
  92.9 54.6 %all-to-all-start = ((bf16[16,4,2,16,512]{4,3,2,1,0:T(8,128)(2,1)}), bf16[16,4,2,16,512]{4,3,2,1,0:T(8,128)(2,1)S(1)}, u32[]{:S(2)}, u32[]{:S(2)}) async-start(bf16[16,4,2,16,512]{4,3,2,1,0:T(8,128)(2,1)} %bitcast.7), calls=%async_computation | async-start | bytes 4194304 | tf_op jit(solution)/shard_map/all_to_all | solution.py:192
  98.0 48.2 %collective-permute-start.3 = (bf16[16,4,2,16,512]{4,3,2,1,0:T(8,128)(2,1)}, bf16[16,4,2,16,512]{4,3,2,1,0:T(8,128)(2,1)S(1)}, u32[]{:S(2)}, u32[]{:S(2)}) collective-permute-start(bf16[16,4,2,16,512]{4,3,2,1,0:T(8,128)(2,1)} %all_to_all.20.own_ref), channel_id=1, source_target_pairs={{0,16},{16,0},{1,17},{17,1},{2,18},{18,2},{3,19},{19,3},{4,20},{20... | collective-permute-start | bytes 6291464 | tf_op jit(solution)/shard_map/ppermute | solution.py:25
  146.2 1.4 copy-start.3
  147.5 5.8 %copy-start = (bf16[16,4,2,16,512]{4,3,2,1,0:T(8,128)(2,1)}, bf16[16,4,2,16,512]{4,3,2,1,0:T(8,128)(2,1)S(1)}, u32[]{:S(2)}) copy-start(bf16[16,4,2,16,512]{4,3,2,1,0:T(8,128)(2,1)S(1)} %all-to-all-done.own_ref) | copy-start | bytes 6291460
  147.5 55.1 %all-to-all-start.3 = ((bf16[16,4,2,16,512]{4,3,2,1,0:T(8,128)(2,1)}), bf16[16,4,2,16,512]{4,3,2,1,0:T(8,128)(2,1)}, u32[]{:S(2)}, u32[]{:S(2)}) async-start(bf16[16,4,2,16,512]{4,3,2,1,0:T(8,128)(2,1)} %bitcast.6), calls=%async_computation.3 | async-start | bytes 4194304 | tf_op jit(solution)/shard_map/all_to_all | solution.py:192
  153.3 48.0 %collective-permute-start.1 = (bf16[16,4,2,16,512]{4,3,2,1,0:T(8,128)(2,1)S(1)}, bf16[16,4,2,16,512]{4,3,2,1,0:T(8,128)(2,1)S(1)}, u32[]{:S(2)}, u32[]{:S(2)}) collective-permute-start(bf16[16,4,2,16,512]{4,3,2,1,0:T(8,128)(2,1)S(1)} %all-to-all-done.own_ref), channel_id=1, source_target_pairs={{0,16},{16,0},{1,17},{17,1},{2,18},{18,2},{3,19},{19,3},{4,20},{20... | collective-permute-start | bytes 6291464 | tf_op jit(solution)/shard_map/ppermute | solution.py:25
  201.3 1.3 copy-start.2
  202.6 46.9 %all-to-all-start.1 = ((bf16[16,4,2,16,512]{4,3,2,1,0:T(8,128)(2,1)}), bf16[16,4,2,16,512]{4,3,2,1,0:T(8,128)(2,1)S(1)}, u32[]{:S(2)}, u32[]{:S(2)}) async-start(bf16[16,4,2,16,512]{4,3,2,1,0:T(8,128)(2,1)} %bitcast.5), calls=%async_computation.1 | async-start | bytes 4194304 | tf_op jit(solution)/shard_map/all_to_all | solution.py:192
  208.4 62.9 %collective-permute-start.4 = (bf16[16,4,2,16,512]{4,3,2,1,0:T(8,128)(2,1)}, bf16[16,4,2,16,512]{4,3,2,1,0:T(8,128)(2,1)}, u32[]{:S(2)}, u32[]{:S(2)}) collective-permute-start(bf16[16,4,2,16,512]{4,3,2,1,0:T(8,128)(2,1)} %all-to-all-done.3.own_ref), channel_id=1, source_target_pairs={{0,16},{16,0},{1,17},{17,1},{2,18},{18,2},{3,19},{19,3},{4,20},{20... | collective-permute-start | bytes 6291464 | tf_op jit(solution)/shard_map/ppermute | solution.py:25
  249.5 11.6 %copy-start.1 = (bf16[16,4,2,16,512]{4,3,2,1,0:T(8,128)(2,1)}, bf16[16,4,2,16,512]{4,3,2,1,0:T(8,128)(2,1)S(1)}, u32[]{:S(2)}) copy-start(bf16[16,4,2,16,512]{4,3,2,1,0:T(8,128)(2,1)S(1)} %all-to-all-done.1.own_ref) | copy-start | bytes 6291460
  249.5 52.2 %collective-permute-start.2 = (bf16[16,4,2,16,512]{4,3,2,1,0:T(8,128)(2,1)S(1)}, bf16[16,4,2,16,512]{4,3,2,1,0:T(8,128)(2,1)}, u32[]{:S(2)}, u32[]{:S(2)}) collective-permute-start(bf16[16,4,2,16,512]{4,3,2,1,0:T(8,128)(2,1)S(1)} %all-to-all-done.1.own_ref), channel_id=1, source_target_pairs={{0,16},{16,0},{1,17},{17,1},{2,18},{18,2},{3,19},{19,3},{4,20},{20... | collective-permute-start | bytes 6291464 | tf_op jit(solution)/shard_map/ppermute | solution.py:25

commit v2 on v0

v2 whole, which is shorter than its diff:
```python
import functools
import math

import jax
import jax.numpy as jnp
import numpy as np
from jax import lax
from jax.experimental import pallas as pl
from jax.experimental.pallas import tpu as pltpu
from jax.sharding import PartitionSpec as P

VMEM_LIMIT = 56 << 20
HALVES = 2
CUT = 1
OWN_AT = 1
OTHER_AT = 4
FIRST = 2
XLAG = 3
ZORD = (1, 3, 2)
FAR = 3


def after(value, earlier):
    return lax.optimization_barrier((value, *earlier))[0] if earlier else value


def from_behind(value, axis):
    devices = lax.axis_size(axis)
    return lax.ppermute(value, axis, [(i, i + 1) for i in range(devices - 1)])


def from_partner(value, axis, by):
    return lax.ppermute(value, axis, [(i, i ^ by) for i in range(lax.axis_size(axis))])


def dft_rows(length, devices, halves):
    channels = length // 2
    part = channels // devices // halves
    k = np.arange(channels).reshape(devices, halves, part).transpose(1, 0, 2)[..., None]
    phase = (k * np.arange(length) % length) * (2.0 * math.pi / length)
    norm = 1.0 / math.sqrt(length)
    table = np.stack([np.cos(phase) * norm, -np.sin(phase) * norm], axis=3)
    return jnp.asarray(table.reshape(halves, devices, 2 * part, length), jnp.bfloat16)


def filtered(taps, frame, s):
    total = taps[0:1] * frame(s)
    for t in range(1, taps.shape[0]):
        total = total + taps[t : t + 1] * frame(s + t)
    return total.astype(jnp.bfloat16)


def transform(table, values):
    return lax.dot_general(
        table, values, (((1,), (1,)), ((), ())), preferred_element_type=jnp.float32
    ).astype(jnp.bfloat16)


def place_table(here_ref, table_ref, table):
    halves, devices, rows, _ = table_ref.shape

    @pl.when(pl.program_id(0) == 0)
    def _():
        for h in range(halves):
            for d in range(devices):
                at = (h * devices + d) * rows
                table[at : at + rows] = table_ref[h, here_ref[0] ^ d]


def late_body(here_ref, taps_ref, table_ref, raw_ref, out_ref, table):
    length = taps_ref.shape[1]
    taps = taps_ref[...]
    place_table(here_ref, table_ref, table)

    def frame(f):
        return raw_ref[:, f * length : (f + 1) * length].astype(jnp.float32)

    for s in range(out_ref.shape[0]):
        out_ref[s] = transform(table[...], filtered(taps, frame, s))


def pieces_body(group, here_ref, taps_ref, table_ref, order_ref, late_ref, raw_ref, halo_ref, *refs):
    *outs, table = refs
    n_taps, length = taps_ref.shape
    width = raw_ref.shape[0]
    early = n_taps - 1
    frames = early + late_ref.shape[0]
    rows = table_ref.shape[2]
    taps = taps_ref[...]
    place_table(here_ref, table_ref, table)

    def frame(f):
        ref, at = (halo_ref, f) if f < early else (raw_ref, f - early)
        return ref[:, at * length : (at + 1) * length].astype(jnp.float32)

    first_ones = [transform(table[...], filtered(taps, frame, s)) for s in range(early)]
    for first in range(0, table.shape[0], group):
        mixed = [one[first : first + group] for one in first_ones]
        mixed += [late_ref[s, first : first + group] for s in range(frames - early)]
        turned = jnp.dot(
            order_ref[...], jnp.concatenate(mixed, axis=0), preferred_element_type=jnp.float32
        )
        turned = turned.astype(jnp.bfloat16).reshape(group, frames, width)
        step = min(group, rows)
        for at in range(0, group, step):
            piece, row = divmod(first + at, rows)
            outs[piece][row // 2 : (row + step) // 2] = turned[at : at + step].reshape(
                step // 2, 2, frames, width
            )


def late_spectra(here, raw, taps, table, frames):
    n_taps, length = taps.shape
    inputs, samples = raw.shape
    block = min(inputs, 256)
    late = frames - (n_taps - 1)
    return pl.pallas_call(
        late_body,
        grid_spec=pltpu.PrefetchScalarGridSpec(
            num_scalar_prefetch=1,
            grid=(inputs // block,),
            in_specs=[
                pl.BlockSpec(taps.shape, lambda i, t: (0, 0)),
                pl.BlockSpec(table.shape, lambda i, t: (0, 0, 0, 0)),
                pl.BlockSpec((block, samples), lambda i, t: (i, 0)),
            ],
            out_specs=pl.BlockSpec((late, length, block), lambda i, t: (0, 0, i)),
            scratch_shapes=[pltpu.VMEM((length, length), jnp.bfloat16)],
        ),
        out_shape=jax.ShapeDtypeStruct((late, length, inputs), jnp.bfloat16),
        compiler_params=pltpu.CompilerParams(vmem_limit_bytes=VMEM_LIMIT),
        cost_estimate=pl.CostEstimate(
            flops=2 * inputs * samples * length, bytes_accessed=4 * inputs * samples, transcendentals=0
        ),
        name="late_spectra",
    )(here, taps, table, raw)


def make_pieces(h, here, late, raw, halo, taps, table):
    halves, devices, rows, length = table.shape
    inputs = raw.shape[0]
    frames = late.shape[0] + taps.shape[0] - 1
    block = min(inputs, 256)
    group = 16
    order = np.zeros((group, frames, frames, group), np.float32)
    for r in range(group):
        for s in range(frames):
            order[r, s, s, r] = 1.0
    order = jnp.asarray(order.reshape(group * frames, group * frames), jnp.bfloat16)
    edge = pl.BlockSpec((block, halo.shape[1]), lambda i, t: (i, 0))
    outs = pl.pallas_call(
        functools.partial(pieces_body, group),
        grid_spec=pltpu.PrefetchScalarGridSpec(
            num_scalar_prefetch=1,
            grid=(inputs // block,),
            in_specs=[
                pl.BlockSpec(taps.shape, lambda i, t: (0, 0)),
                pl.BlockSpec((1, devices, rows, length), lambda i, t: (h, 0, 0, 0)),
                pl.BlockSpec(order.shape, lambda i, t: (0, 0)),
                pl.BlockSpec((late.shape[0], devices * rows, block), lambda i, t: (0, h, i)),
                edge,
                edge,
            ],
            out_specs=[
                pl.BlockSpec((rows // 2, 2, frames, block), lambda i, t: (0, 0, 0, i))
            ] * devices,
            scratch_shapes=[pltpu.VMEM((devices * rows, length), jnp.bfloat16)],
        ),
        out_shape=[jax.ShapeDtypeStruct((rows // 2, 2, frames, inputs), jnp.bfloat16)] * devices,
        compiler_params=pltpu.CompilerParams(vmem_limit_bytes=VMEM_LIMIT),
        cost_estimate=pl.CostEstimate(
            flops=4 * inputs * frames * devices * rows * group * frames // 2,
            bytes_accessed=4 * inputs * frames * devices * rows,
            transcendentals=0,
        ),
        name="pieces",
    )(here, taps, table, order, late, raw, halo)
    return dict(enumerate(outs))


def correlate_body(count, n, crossed, group_ref, *refs):
    out_ref, token_ref = refs[-2:]
    frames, inputs = refs[0].shape[2:]

    def parts(pieces):
        return [
            jnp.concatenate([piece[0, r] for piece in pieces], axis=0) for r in range(2)
        ]

    own = parts(refs[:n])
    real, imag = parts(refs[n : 2 * n]) if crossed else own
    rows = jnp.transpose(jnp.concatenate(own, axis=0))
    for which, pair in enumerate(((real, imag), (imag, -real))):
        product = jnp.dot(rows, jnp.concatenate(pair, axis=0), preferred_element_type=jnp.float32)
        out_ref[0, which] = product * (1.0 / count)
    token_ref[...] = jnp.zeros_like(token_ref)


def correlate(group, own, other, earlier, shape, first, start, channels, count):
    n = len(own)
    _, _, frames, inputs = own[0].shape
    pieces = own + (other or [])
    held = [] if earlier is None else [earlier]
    crossed = other is not None
    spec = pl.BlockSpec((1, 2, frames, inputs), lambda c, g: (start + c, 0, 0, 0))
    return pl.pallas_call(
        functools.partial(correlate_body, count, n, crossed),
        grid_spec=pltpu.PrefetchScalarGridSpec(
            num_scalar_prefetch=1,
            grid=(channels,),
            in_specs=[spec] * len(pieces) + [pl.BlockSpec(memory_space=pl.ANY)] * len(held),
            out_specs=[
                pl.BlockSpec(
                    (1, 2, inputs, inputs),
                    lambda c, g: (first + start + c, 0, 0, 1 - g[0] if crossed else g[0]),
                ),
                pl.BlockSpec((8, 128), lambda c, g: (0, 0)),
            ],
        ),
        out_shape=[
            jax.ShapeDtypeStruct(shape, jnp.float32),
            jax.ShapeDtypeStruct((8, 128), jnp.float32),
        ],
        input_output_aliases={1 + len(pieces): 0} if held else {},
        compiler_params=pltpu.CompilerParams(vmem_limit_bytes=VMEM_LIMIT),
        cost_estimate=pl.CostEstimate(
            flops=channels * 8 * inputs * inputs * n * frames,
            bytes_accessed=channels * 4 * inputs * (2 * inputs + 2 * n * frames),
            transcendentals=0,
        ),
        name="correlate_other" if crossed else "correlate_own",
    )(group, *pieces, *held)


def turn_orders(devices):
    near = max(1, devices // 4)
    far = [q + near * z for q in range(near) for z in ZORD if q + near * z < devices]
    close = list(range(1, near))
    return far, close, list(range(near)) + far


def per_device(raw, taps):
    n_taps, length = taps.shape
    inputs, samples = raw.shape
    devices = lax.axis_size("tm")
    own_channels = length // 2 // devices
    count = samples // length * devices
    halves = HALVES if own_channels % HALVES == 0 else 1
    part = own_channels // halves
    halo = from_behind(raw[:, samples - (n_taps - 1) * length :], "tm")
    here = lax.axis_index("tm")[None]
    table = dft_rows(length, devices, halves)
    late = late_spectra(here, raw, taps, table, samples // length)
    group = lax.axis_index("inp")[None]
    shape = (own_channels, 2, inputs, inputs * lax.axis_size("inp"))

    far, close, order = turn_orders(devices)
    come, others, tokens = {}, {}, []
    far_chain, close_chain, chain = [], [], []
    result = None

    def send(key, value, sent, lag, axis, by, arrived, more=()):
        earlier = [arrived[sent[-lag]]] if len(sent) >= lag else []
        arrived[key] = from_partner(after(value, earlier + list(more)), axis, by)
        sent.append(key)

    for h in range(halves):
        wait = [others[0, order[0]]] if h else []
        spectra = make_pieces(h, here, after(late, wait), raw, halo, taps, table)
        come[h, 0] = spectra[0]
        if not h:
            send((h, 0), come[h, 0], chain, XLAG, "inp", 1, others)
        for k, d in enumerate(far):
            more = [others[0, 0]] if FIRST == k and not h else []
            send((h, d), spectra[d], far_chain, FAR, "tm", d, come, more)
        for d in close:
            send((h, d), spectra[d], close_chain, 1, "tm", d, come)
        for k, d in enumerate(order):
            if (h, d) in others:
                continue
            more = [token for at, token in zip((OWN_AT, OTHER_AT), tokens) if at == k]
            send((h, d), come[h, d], chain, XLAG, "inp", 1, others, more)
        own = [come[h, d] for d in range(devices)]
        other = [others[h, d] for d in range(devices)]
        tokens = []
        cut = max(1, part // CUT)
        for crossed in (None, other):
            for start in range(0, part, cut):
                result, token = correlate(
                    group, own, crossed, result, shape, h * part, start, min(cut, part - start), count
                )
                tokens.append(token)
    return result


def solution(mesh):
    return jax.shard_map(
        per_device,
        mesh=mesh,
        in_specs=(P("inp", "tm"), P()),
        out_specs=P("tm", None, "inp", None),
        check_vma=False,
    )
```

time: 604 us -> 276 us (0.46)
  blocking collectives: 206 us -> 0 us
  starting transfers between devices: 3.94 us -> 102 us
  waiting for transfers between devices: 183 us -> 93 us
  local copies, waits for them, and re-layouts: 87.4 us -> 3.69 us
  Pallas kernels: 0 us -> 72 us
  matrix products: 63.9 us -> 0 us
  other arithmetic: 60.1 us -> 0 us
    all_to_all x1 -> x0, blocking collectives: 206 us -> none  [per_device(): lax.all_to_all(spectra, 'tm', split_axis=0, concat_axis=2, tiled=True)]
    ppermute x2 -> x63, starting transfers between devices: 3.94 us -> 102 us  [the longest x62 99.8 us: from_partner(): lax.ppermute(value, axis, [(i, i ^ by) for i in range(lax.axis_size(axis))])]
    ppermute x2 -> x63, waiting for transfers between devices: 183 us -> 93 us  [the longest x62 93 us: from_partner(): lax.ppermute(value, axis, [(i, i ^ by) for i in range(lax.axis_size(axis))])]
    pallas_call x0 -> x7, Pallas kernels: none -> 72 us  [the longest x4 48.2 us: correlate(): pl.pallas_call(functools.partial(correlate_body, count, n, crossed), grid...]
    dot_general x3 -> x0, matrix products: 63.9 us -> none  [the longest x1 24.3 us: cross_power(): jnp.einsum('crsi,crsj->cij', rows, cols, preferred_element_type=jnp.float32)]
    div x1 -> x0, other arithmetic: 44.5 us -> none  [cross_power(): return jnp.stack([real_part, imag_part], axis=1) / count]
    div x1 -> x0, local copies, waits for them, and re-layouts: 43.8 us -> none  [cross_power(): return jnp.stack([real_part, imag_part], axis=1) / count]
    convert_element_type x1 -> x0, local copies, waits for them, and re-layouts: 11.5 us -> none  [per_device(): spectra = jnp.einsum('isn,crn->crsi', filtered, table, preferred_element_...]
  transfers between devices with their start and end apart: 2 -> 63, of which waited for: 2 -> 22; matrix products, arithmetic and copies ran while one was open for 0% -> 0% of each run, Pallas kernels for 0% -> 20%
where the time goes in v2:
time: 276 us; the launch traced here: 272 us
  starting transfers between devices  102 us (37%)
  waiting for transfers between devices  93 us (34%)
  Pallas kernels  72 us (26%)
  local copies, waits for them, and re-layouts  3.69 us (1%)
    ppermute x62, starting transfers between devices, from_partner(): lax.ppermute(value, axis, [(i, i ^ by) for i in range(lax.axis_size(axis))])  99.8 us
    ppermute x62, waiting for transfers between devices, from_partner(): lax.ppermute(value, axis, [(i, i ^ by) for i in range(lax.axis_size(axis))])  93 us
    pallas_call x4, Pallas kernels, correlate(): pl.pallas_call(functools.partial(correlate_body, count, n, crossed), grid...  48.2 us
    pallas_call x2, Pallas kernels, make_pieces(): pl.pallas_call(functools.partial(pieces_body, group), grid_spec=pltpu.Pre...  12.4 us
    pallas_call x1, Pallas kernels, late_spectra(): pl.pallas_call(late_body, grid_spec=pltpu.PrefetchScalarGridSpec(num_scal...  11.4 us
  transfers between devices with their start and end apart: 63, of which 22 were waited for; matrix products, arithmetic and copies ran while one was open for 0% of the time, Pallas kernels for 20%

profile of v2, /device:TPU:0, one launch (start us, length us, event | category | flops | bytes accessed | tf_op | source)
XLA Modules:
  0.0 271.8 jit_solution(8647776913919141945)
XLA Ops:
  0.0 1.5 slice.3
  1.5 2.5 collective-permute-start
  4.0 11.4 %late_spectra.1.late_ref = bf16[13,512,512]{2,1,0:T(8,128)(2,1)} custom-call(s32[1]{0:T(128)} %bitcast.1.here_ref, f32[4,512]{1,0:T(4,128)} %taps_ref.5, bf16[2,16,16,512]{3,2,1,0:T(8,128)(2,1)} %constant.13.clone.table_ref, bf16[512,8192]{1,0:T(8,128)(2,1)} %raw_ref.5), custom_call_target="tpu_custom_call" | custom-call | flops 4294967296 | bytes 16777216 | tf_op jit(solution)/shard_map/late_spectra/pallas_call | solution.py:117
  16.5 6.2 %pieces.2 = (bf16[8,2,16,512]{3,2,1,0:T(8,128)(2,1)}, bf16[8,2,16,512]{3,2,1,0:T(8,128)(2,1)}, bf16[8,2,16,512]{3,2,1,0:T(8,128)(2,1)}, bf16[8,2,16,512]{3,2,1,0...) custom-call(s32[1]{0:T(128)} %bitcast.1.here_ref, ...), custom_call_target="tpu_custom_call" | custom-call | flops 1073741824 | bytes 8388608 | tf_op jit(solution)/shard_map/pieces/pallas_call | solution.py:151
  22.7 8.5 %collective-permute-start.2 = (bf16[8,2,16,512]{3,2,1,0:T(8,128)(2,1)}, bf16[8,2,16,512]{3,2,1,0:T(8,128)(2,1)S(1)}, u32[]{:S(2)}, u32[]{:S(2)}) collective-permute-start(bf16[8,2,16,512]{3,2,1,0:T(8,128)(2,1)} %get-tuple-element.104), channel_id=1, source_target_pairs={{0,1},{1,0},{2,3},{3,2},{4,5},{5,4},{6,7},{7,6},{8,9},{9,8},{10,11... | collective-permute-start | bytes 786440 | tf_op jit(solution)/shard_map/ppermute | solution.py:33
  32.6 2.7 %collective-permute-start.3 = (bf16[8,2,16,512]{3,2,1,0:T(8,128)(2,1)}, bf16[8,2,16,512]{3,2,1,0:T(8,128)(2,1)S(1)}, u32[]{:S(2)}, u32[]{:S(2)}) collective-permute-start(bf16[8,2,16,512]{3,2,1,0:T(8,128)(2,1)} %get-tuple-element.105), channel_id=1, source_target_pairs={{0,2},{1,3},{2,0},{3,1},{4,6},{5,7},{6,4},{7,5},{8,10},{9,11},{10,... | collective-permute-start | bytes 786440 | tf_op jit(solution)/shard_map/ppermute | solution.py:33
  35.4 1.6 collective-permute-start.8
  37.0 2.5 collective-permute-start.24
  45.2 7.3 %collective-permute-done.24.refs_12_ = bf16[8,2,16,512]{3,2,1,0:T(8,128)(2,1)S(1)} collective-permute-done((bf16[8,2,16,512]{3,2,1,0:T(8,128)(2,1)}, bf16[8,2,16,512]{3,2,1,0:T(8,128)(2,1)S(1)}, u32[]{:S(2)}, u32[]{:S(2)}) %collective-permute-start.24) | collective-permute-done | bytes 262176 | tf_op jit(solution)/shard_map/ppermute | solution.py:33
  52.5 1.6 collective-permute-start.38
  55.3 1.6 collective-permute-done.9.refs_5_
  58.4 4.9 %collective-permute-done.25.refs_13_ = bf16[8,2,16,512]{3,2,1,0:T(8,128)(2,1)S(1)} collective-permute-done((bf16[8,2,16,512]{3,2,1,0:T(8,128)(2,1)}, bf16[8,2,16,512]{3,2,1,0:T(8,128)(2,1)S(1)}, u32[]{:S(2)}, u32[]{:S(2)}) %collective-permute-start.25) | collective-permute-done | bytes 262176 | tf_op jit(solution)/shard_map/ppermute | solution.py:33
  63.3 8.3 %collective-permute-start.10 = (bf16[8,2,16,512]{3,2,1,0:T(8,128)(2,1)}, bf16[8,2,16,512]{3,2,1,0:T(8,128)(2,1)S(1)}, u32[]{:S(2)}, u32[]{:S(2)}) collective-permute-start(bf16[8,2,16,512]{3,2,1,0:T(8,128)(2,1)} %get-tuple-element.118), channel_id=1, source_target_pairs={{0,6},{1,7},{2,4},{3,5},{4,2},{5,3},{6,0},{7,1},{8,14},{9,15},{10,... | collective-permute-start | bytes 786440 | tf_op jit(solution)/shard_map/ppermute | solution.py:33
  71.6 3.9 %collective-permute-start.26 = (bf16[8,2,16,512]{3,2,1,0:T(8,128)(2,1)}, bf16[8,2,16,512]{3,2,1,0:T(8,128)(2,1)S(1)}, u32[]{:S(2)}, u32[]{:S(2)}) collective-permute-start(bf16[8,2,16,512]{3,2,1,0:T(8,128)(2,1)} %get-tuple-element.149), channel_id=1, source_target_pairs={{0,14},{1,15},{2,12},{3,13},{4,10},{5,11},{6,8},{7,9},{8,6},{9,7},... | collective-permute-start | bytes 786440 | tf_op jit(solution)/shard_map/ppermute | solution.py:33
  75.6 1.5 collective-permute-start.39
  77.4 1.5 collective-permute-start.34
  78.9 9.2 %collective-permute-done.10.refs_6_ = bf16[8,2,16,512]{3,2,1,0:T(8,128)(2,1)S(1)} collective-permute-done((bf16[8,2,16,512]{3,2,1,0:T(8,128)(2,1)}, bf16[8,2,16,512]{3,2,1,0:T(8,128)(2,1)S(1)}, u32[]{:S(2)}, u32[]{:S(2)}) %collective-permute-start.10) | collective-permute-done | bytes 262176 | tf_op jit(solution)/shard_map/ppermute | solution.py:33
  89.6 6.2 %pieces.3 = (bf16[8,2,16,512]{3,2,1,0:T(8,128)(2,1)}, bf16[8,2,16,512]{3,2,1,0:T(8,128)(2,1)}, bf16[8,2,16,512]{3,2,1,0:T(8,128)(2,1)}, bf16[8,2,16,512]{3,2,1,0...) custom-call(s32[1]{0:T(128)} %bitcast.1.here_ref, ...), custom_call_target="tpu_custom_call" | custom-call | flops 1073741824 | bytes 8388608 | tf_op jit(solution)/shard_map/pieces/pallas_call | solution.py:151
  96.0 1.5 collective-permute-start.5
  101.3 1.6 collective-permute-start.18
  102.9 3.4 %collective-permute-done.11.refs_7_ = bf16[8,2,16,512]{3,2,1,0:T(8,128)(2,1)S(1)} collective-permute-done((bf16[8,2,16,512]{3,2,1,0:T(8,128)(2,1)}, bf16[8,2,16,512]{3,2,1,0:T(8,128)(2,1)S(1)}, u32[]{:S(2)}, u32[]{:S(2)}) %collective-permute-start.11) | collective-permute-done | bytes 262176 | tf_op jit(solution)/shard_map/ppermute | solution.py:33
  106.3 2.4 collective-permute-start.46
  108.7 3.6 %collective-permute-start.27 = (bf16[8,2,16,512]{3,2,1,0:T(8,128)(2,1)}, bf16[8,2,16,512]{3,2,1,0:T(8,128)(2,1)S(1)}, u32[]{:S(2)}, u32[]{:S(2)}) collective-permute-start(bf16[8,2,16,512]{3,2,1,0:T(8,128)(2,1)} %get-tuple-element.150), channel_id=1, source_target_pairs={{0,15},{1,14},{2,13},{3,12},{4,11},{5,10},{6,9},{7,8},{8,7},{9,6},... | collective-permute-start | bytes 786440 | tf_op jit(solution)/shard_map/ppermute | solution.py:33
  113.7 9.9 %collective-permute-done.18.refs_10_ = bf16[8,2,16,512]{3,2,1,0:T(8,128)(2,1)S(1)} collective-permute-done((bf16[8,2,16,512]{3,2,1,0:T(8,128)(2,1)}, bf16[8,2,16,512]{3,2,1,0:T(8,128)(2,1)S(1)}, u32[]{:S(2)}, u32[]{:S(2)}) %collective-permute-start.18) | collective-permute-done | bytes 262176 | tf_op jit(solution)/shard_map/ppermute | solution.py:33
  125.8 3.3 %collective-permute-done.6.refs_2_ = bf16[8,2,16,512]{3,2,1,0:T(8,128)(2,1)S(1)} collective-permute-done((bf16[8,2,16,512]{3,2,1,0:T(8,128)(2,1)}, bf16[8,2,16,512]{3,2,1,0:T(8,128)(2,1)S(1)}, u32[]{:S(2)}, u32[]{:S(2)}) %collective-permute-start.6) | collective-permute-done | bytes 262176 | tf_op jit(solution)/shard_map/ppermute | solution.py:33
  129.1 6.5 %collective-permute-start.12 = (bf16[8,2,16,512]{3,2,1,0:T(8,128)(2,1)}, bf16[8,2,16,512]{3,2,1,0:T(8,128)(2,1)S(1)}, u32[]{:S(2)}, u32[]{:S(2)}) collective-permute-start(bf16[8,2,16,512]{3,2,1,0:T(8,128)(2,1)} %get-tuple-element.120), channel_id=1, source_target_pairs={{0,4},{1,5},{2,6},{3,7},{4,0},{5,1},{6,2},{7,3},{8,12},{9,13},{10,... | collective-permute-start | bytes 786440 | tf_op jit(solution)/shard_map/ppermute | solution.py:33
  135.7 1.6 collective-permute-start.42
  137.3 3.0 %collective-permute-done.19.refs_11_ = bf16[8,2,16,512]{3,2,1,0:T(8,128)(2,1)S(1)} collective-permute-done((bf16[8,2,16,512]{3,2,1,0:T(8,128)(2,1)}, bf16[8,2,16,512]{3,2,1,0:T(8,128)(2,1)S(1)}, u32[]{:S(2)}, u32[]{:S(2)}) %collective-permute-start.19) | collective-permute-done | bytes 262176 | tf_op jit(solution)/shard_map/ppermute | solution.py:33
  140.7 1.6 collective-permute-start.48
  142.3 2.7 %collective-permute-done.12.refs_4_ = bf16[8,2,16,512]{3,2,1,0:T(8,128)(2,1)S(1)} collective-permute-done((bf16[8,2,16,512]{3,2,1,0:T(8,128)(2,1)}, bf16[8,2,16,512]{3,2,1,0:T(8,128)(2,1)S(1)}, u32[]{:S(2)}, u32[]{:S(2)}) %collective-permute-start.12) | collective-permute-done | bytes 262176 | tf_op jit(solution)/shard_map/ppermute | solution.py:33
  145.0 1.8 collective-permute-start.28
  146.9 2.8 %collective-permute-start.20 = (bf16[8,2,16,512]{3,2,1,0:T(8,128)(2,1)}, bf16[8,2,16,512]{3,2,1,0:T(8,128)(2,1)S(1)}, u32[]{:S(2)}, u32[]{:S(2)}) collective-permute-start(bf16[8,2,16,512]{3,2,1,0:T(8,128)(2,1)} %get-tuple-element.136), channel_id=1, source_target_pairs={{0,8},{1,9},{2,10},{3,11},{4,12},{5,13},{6,14},{7,15},{8,0},{9,1},... | collective-permute-start | bytes 786440 | tf_op jit(solution)/shard_map/ppermute | solution.py:33
  152.0 4.2 %collective-permute-done.48.refs_27_ = bf16[8,2,16,512]{3,2,1,0:T(8,128)(2,1)} collective-permute-done((bf16[8,2,16,512]{3,2,1,0:T(8,128)(2,1)S(1)}, bf16[8,2,16,512]{3,2,1,0:T(8,128)(2,1)}, u32[]{:S(2)}, u32[]{:S(2)}) %collective-permute-start.48) | collective-permute-done | bytes 262176 | tf_op jit(solution)/shard_map/ppermute | solution.py:33
  158.3 5.6 %collective-permute-done.13.refs_5_ = bf16[8,2,16,512]{3,2,1,0:T(8,128)(2,1)S(1)} collective-permute-done((bf16[8,2,16,512]{3,2,1,0:T(8,128)(2,1)}, bf16[8,2,16,512]{3,2,1,0:T(8,128)(2,1)S(1)}, u32[]{:S(2)}, u32[]{:S(2)}) %collective-permute-start.13) | collective-permute-done | bytes 262176 | tf_op jit(solution)/shard_map/ppermute | solution.py:33
  165.4 10.6 %collective-permute-done.20.refs_8_ = bf16[8,2,16,512]{3,2,1,0:T(8,128)(2,1)S(1)} collective-permute-done((bf16[8,2,16,512]{3,2,1,0:T(8,128)(2,1)}, bf16[8,2,16,512]{3,2,1,0:T(8,128)(2,1)S(1)}, u32[]{:S(2)}, u32[]{:S(2)}) %collective-permute-start.20) | collective-permute-done | bytes 262176 | tf_op jit(solution)/shard_map/ppermute | solution.py:33
  176.1 1.7 collective-permute-start.51
  178.3 1.7 collective-permute-start.59
  179.9 4.8 %collective-permute-done.14.refs_6_ = bf16[8,2,16,512]{3,2,1,0:T(8,128)(2,1)S(1)} collective-permute-done((bf16[8,2,16,512]{3,2,1,0:T(8,128)(2,1)}, bf16[8,2,16,512]{3,2,1,0:T(8,128)(2,1)S(1)}, u32[]{:S(2)}, u32[]{:S(2)}) %collective-permute-start.14) | collective-permute-done | bytes 262176 | tf_op jit(solution)/shard_map/ppermute | solution.py:33
  184.8 2.9 %collective-permute-start.30 = (bf16[8,2,16,512]{3,2,1,0:T(8,128)(2,1)}, bf16[8,2,16,512]{3,2,1,0:T(8,128)(2,1)S(1)}, u32[]{:S(2)}, u32[]{:S(2)}) collective-permute-start(bf16[8,2,16,512]{3,2,1,0:T(8,128)(2,1)} %get-tuple-element.155), channel_id=1, source_target_pairs={{0,14},{1,15},{2,12},{3,13},{4,10},{5,11},{6,8},{7,9},{8,6},{9,7},... | collective-permute-start | bytes 786440 | tf_op jit(solution)/shard_map/ppermute | solution.py:33
  187.8 9.4 %collective-permute-done.21.refs_9_ = bf16[8,2,16,512]{3,2,1,0:T(8,128)(2,1)S(1)} collective-permute-done((bf16[8,2,16,512]{3,2,1,0:T(8,128)(2,1)}, bf16[8,2,16,512]{3,2,1,0:T(8,128)(2,1)S(1)}, u32[]{:S(2)}, u32[]{:S(2)}) %collective-permute-start.21) | collective-permute-done | bytes 262176 | tf_op jit(solution)/shard_map/ppermute | solution.py:33
  197.2 3.7 %collective-permute-start.22 = (bf16[8,2,16,512]{3,2,1,0:T(8,128)(2,1)}, bf16[8,2,16,512]{3,2,1,0:T(8,128)(2,1)S(1)}, u32[]{:S(2)}, u32[]{:S(2)}) collective-permute-start(bf16[8,2,16,512]{3,2,1,0:T(8,128)(2,1)} %get-tuple-element.140), channel_id=1, source_target_pairs={{0,10},{1,11},{2,8},{3,9},{4,14},{5,15},{6,12},{7,13},{8,2},{9,3},... | collective-permute-start | bytes 786440 | tf_op jit(solution)/shard_map/ppermute | solution.py:33
  203.6 11.3 %correlate_own.2 = (f32[16,2,512,1024]{3,2,1,0:T(8,128)}, f32[8,128]{1,0:T(8,128)}) custom-call(s32[1]{0:T(128)} %bitcast.group_ref, bf16[8,2,16,512]{3,2,1,0:T(8,128)(2,1)} %get-tuple-element.98.refs_0_, bf16[8,2,16,512]{3,2,1,0:T(8,128)(2,1)} %copy-done.16, bf16[8,2,16,512]{3,2,1,0:T(8,128)(2,1)} %copy-done.17, bf16[8,2,16,512]{3,2,1,0:T(8,128)(2,1)} %copy-done.22, ...), custom_call_target="tpu_custom_call" | custom-call | flops 4294967296 | bytes 25165824 | tf_op jit(solution)/shard_map/correlate_own/pallas_call | solution.py:206
  214.8 2.0 collective-permute-done.22.refs_10_
  217.9 3.7 %collective-permute-start.23 = (bf16[8,2,16,512]{3,2,1,0:T(8,128)(2,1)}, bf16[8,2,16,512]{3,2,1,0:T(8,128)(2,1)S(1)}, u32[]{:S(2)}, u32[]{:S(2)}) collective-permute-start(bf16[8,2,16,512]{3,2,1,0:T(8,128)(2,1)} %get-tuple-element.142), channel_id=1, source_target_pairs={{0,11},{1,10},{2,9},{3,8},{4,15},{5,14},{6,13},{7,12},{8,3},{9,2},... | collective-permute-start | bytes 786440 | tf_op jit(solution)/shard_map/ppermute | solution.py:33
  225.1 12.9 %correlate_other.2 = (f32[16,2,512,1024]{3,2,1,0:T(8,128)}, f32[8,128]{1,0:T(8,128)}) custom-call(s32[1]{0:T(128)} %bitcast.group_ref, bf16[8,2,16,512]{3,2,1,0:T(8,128)(2,1)} %get-tuple-element.98.refs_0_, bf16[8,2,16,512]{3,2,1,0:T(8,128)(2,1)} %copy-done.16, bf16[8,2,16,512]{3,2,1,0:T(8,128)(2,1)} %copy-done.17, ...), custom_call_target="tpu_custom_call", output_to_operand_aliasing={{0}: (33, {})} | custom-call | flops 4294967296 | bytes 25165824 | tf_op jit(solution)/shard_map/correlate_other/pallas_call | solution.py:206
  238.7 5.7 %collective-permute-done.23.refs_11_ = bf16[8,2,16,512]{3,2,1,0:T(8,128)(2,1)S(1)} collective-permute-done((bf16[8,2,16,512]{3,2,1,0:T(8,128)(2,1)}, bf16[8,2,16,512]{3,2,1,0:T(8,128)(2,1)S(1)}, u32[]{:S(2)}, u32[]{:S(2)}) %collective-permute-start.23) | collective-permute-done | bytes 262176 | tf_op jit(solution)/shard_map/ppermute | solution.py:33
  246.7 11.3 %correlate_own.3 = (f32[16,2,512,1024]{3,2,1,0:T(8,128)}, f32[8,128]{1,0:T(8,128)}) custom-call(s32[1]{0:T(128)} %bitcast.group_ref, bf16[8,2,16,512]{3,2,1,0:T(8,128)(2,1)} %get-tuple-element.162.refs_0_, bf16[8,2,16,512]{3,2,1,0:T(8,128)(2,1)} %copy-done.1, bf16[8,2,16,512]{3,2,1,0:T(8,128)(2,1)} %copy-done.2, ...), custom_call_target="tpu_custom_call", output_to_operand_aliasing={{0}: (17, {})} | custom-call | flops 4294967296 | bytes 25165824 | tf_op jit(solution)/shard_map/correlate_own/pallas_call | solution.py:206
  258.9 12.8 %correlate_other.3 = (f32[16,2,512,1024]{3,2,1,0:T(8,128)}, f32[8,128]{1,0:T(8,128)}) custom-call(s32[1]{0:T(128)} %bitcast.group_ref, bf16[8,2,16,512]{3,2,1,0:T(8,128)(2,1)} %get-tuple-element.162.refs_0_, bf16[8,2,16,512]{3,2,1,0:T(8,128)(2,1)} %copy-done.1, bf16[8,2,16,512]{3,2,1,0:T(8,128)(2,1)} %copy-done.2, ...), custom_call_target="tpu_custom_call", output_to_operand_aliasing={{0}: (33, {})} | custom-call | flops 4294967296 | bytes 25165824 | tf_op jit(solution)/shard_map/correlate_other/pallas_call | solution.py:206
  (204 shorter events, 38.2 us)
Async XLA Ops:
  1.5 13.9 %collective-permute-start = (bf16[512,1536]{1,0:T(8,128)(2,1)S(1)}, bf16[512,1536]{1,0:T(8,128)(2,1)S(1)}, u32[]{:S(2)}, u32[]{:S(2)}) collective-permute-start(bf16[512,1536]{1,0:T(8,128)(2,1)S(1)} %slice.3), channel_id=1, source_target_pairs={{0,1},{1,2},{2,3},{3,4},{4,5},{5,6},{6,7},{7,8},{8,9},{9,10},{10,1... | collective-permute-start | bytes 4718600 | tf_op jit(solution)/shard_map/ppermute | solution.py:29
  37.0 15.6 %collective-permute-start.24 = (bf16[8,2,16,512]{3,2,1,0:T(8,128)(2,1)}, bf16[8,2,16,512]{3,2,1,0:T(8,128)(2,1)S(1)}, u32[]{:S(2)}, u32[]{:S(2)}) collective-permute-start(bf16[8,2,16,512]{3,2,1,0:T(8,128)(2,1)} %get-tuple-element.147), channel_id=1, source_target_pairs={{0,12},{1,13},{2,14},{3,15},{4,8},{5,9},{6,10},{7,11},{8,4},{9,5},... | collective-permute-start | bytes 786440 | tf_op jit(solution)/shard_map/ppermute | solution.py:33
  39.4 13.1 %collective-permute-start.32 = (bf16[8,2,16,512]{3,2,1,0:T(8,128)(2,1)S(1)}, bf16[8,2,16,512]{3,2,1,0:T(8,128)(2,1)S(1)}, u32[]{:S(2)}, u32[]{:S(2)}) collective-permute-start(bf16[8,2,16,512]{3,2,1,0:T(8,128)(2,1)S(1)} %collective-permute-done.2.refs_1_), channel_id=1, source_target_pairs={{0,16},{16,0},{1,17},{17,1},{2,18},{18,2},{3,19},{19,3},{4,20},{20... | collective-permute-start | bytes 786440 | tf_op jit(solution)/shard_map/ppermute | solution.py:33
  40.9 13.2 %collective-permute-start.1 = (bf16[8,2,16,512]{3,2,1,0:T(8,128)(2,1)}, bf16[8,2,16,512]{3,2,1,0:T(8,128)(2,1)S(1)}, u32[]{:S(2)}, u32[]{:S(2)}) collective-permute-start(bf16[8,2,16,512]{3,2,1,0:T(8,128)(2,1)} %get-tuple-element.98.refs_0_), channel_id=1, source_target_pairs={{0,16},{16,0},{1,17},{17,1},{2,18},{18,2},{3,19},{19,3},{4,20},{20... | collective-permute-start | bytes 786440 | tf_op jit(solution)/shard_map/ppermute | solution.py:33
  44.0 13.0 %collective-permute-start.9 = (bf16[8,2,16,512]{3,2,1,0:T(8,128)(2,1)}, bf16[8,2,16,512]{3,2,1,0:T(8,128)(2,1)S(1)}, u32[]{:S(2)}, u32[]{:S(2)}) collective-permute-start(bf16[8,2,16,512]{3,2,1,0:T(8,128)(2,1)} %get-tuple-element.117), channel_id=1, source_target_pairs={{0,5},{1,4},{2,7},{3,6},{4,1},{5,0},{6,3},{7,2},{8,13},{9,12},{10,... | collective-permute-start | bytes 786440 | tf_op jit(solution)/shard_map/ppermute | solution.py:33
  52.5 19.1 %collective-permute-start.38 = (bf16[8,2,16,512]{3,2,1,0:T(8,128)(2,1)S(1)}, bf16[8,2,16,512]{3,2,1,0:T(8,128)(2,1)S(1)}, u32[]{:S(2)}, u32[]{:S(2)}) collective-permute-start(bf16[8,2,16,512]{3,2,1,0:T(8,128)(2,1)S(1)} %collective-permute-done.3.refs_2_), channel_id=1, source_target_pairs={{0,16},{16,0},{1,17},{17,1},{2,18},{18,2},{3,19},{19,3},{4,20},{20... | collective-permute-start | bytes 786440 | tf_op jit(solution)/shard_map/ppermute | solution.py:33
  54.1 21.5 %collective-permute-start.33 = (bf16[8,2,16,512]{3,2,1,0:T(8,128)(2,1)S(1)}, bf16[8,2,16,512]{3,2,1,0:T(8,128)(2,1)S(1)}, u32[]{:S(2)}, u32[]{:S(2)}) collective-permute-start(bf16[8,2,16,512]{3,2,1,0:T(8,128)(2,1)S(1)} %collective-permute-done.8.refs_4_), channel_id=1, source_target_pairs={{0,16},{16,0},{1,17},{17,1},{2,18},{18,2},{3,19},{19,3},{4,20},{20... | collective-permute-start | bytes 786440 | tf_op jit(solution)/shard_map/ppermute | solution.py:33
  54.6 22.8 %collective-permute-start.16 = (bf16[8,2,16,512]{3,2,1,0:T(8,128)(2,1)}, bf16[8,2,16,512]{3,2,1,0:T(8,128)(2,1)S(1)}, u32[]{:S(2)}, u32[]{:S(2)}) collective-permute-start(bf16[8,2,16,512]{3,2,1,0:T(8,128)(2,1)} %get-tuple-element.132), channel_id=1, source_target_pairs={{0,8},{1,9},{2,10},{3,11},{4,12},{5,13},{6,14},{7,15},{8,0},{9,1},... | collective-permute-start | bytes 786440 | tf_op jit(solution)/shard_map/ppermute | solution.py:33
  56.9 22.0 %collective-permute-start.44 = (bf16[8,2,16,512]{3,2,1,0:T(8,128)(2,1)S(1)}, bf16[8,2,16,512]{3,2,1,0:T(8,128)(2,1)S(1)}, u32[]{:S(2)}, u32[]{:S(2)}) collective-permute-start(bf16[8,2,16,512]{3,2,1,0:T(8,128)(2,1)S(1)} %collective-permute-done.4.refs_3_), channel_id=1, source_target_pairs={{0,16},{16,0},{1,17},{17,1},{2,18},{18,2},{3,19},{19,3},{4,20},{20... | collective-permute-start | bytes 786440 | tf_op jit(solution)/shard_map/ppermute | solution.py:33
  63.3 24.8 %collective-permute-start.10 = (bf16[8,2,16,512]{3,2,1,0:T(8,128)(2,1)}, bf16[8,2,16,512]{3,2,1,0:T(8,128)(2,1)S(1)}, u32[]{:S(2)}, u32[]{:S(2)}) collective-permute-start(bf16[8,2,16,512]{3,2,1,0:T(8,128)(2,1)} %get-tuple-element.118), channel_id=1, source_target_pairs={{0,6},{1,7},{2,4},{3,5},{4,2},{5,3},{6,0},{7,1},{8,14},{9,15},{10,... | collective-permute-start | bytes 786440 | tf_op jit(solution)/shard_map/ppermute | solution.py:33
  71.6 24.2 %collective-permute-start.26 = (bf16[8,2,16,512]{3,2,1,0:T(8,128)(2,1)}, bf16[8,2,16,512]{3,2,1,0:T(8,128)(2,1)S(1)}, u32[]{:S(2)}, u32[]{:S(2)}) collective-permute-start(bf16[8,2,16,512]{3,2,1,0:T(8,128)(2,1)} %get-tuple-element.149), channel_id=1, source_target_pairs={{0,14},{1,15},{2,12},{3,13},{4,10},{5,11},{6,8},{7,9},{8,6},{9,7},... | collective-permute-start | bytes 786440 | tf_op jit(solution)/shard_map/ppermute | solution.py:33
  75.6 20.4 %collective-permute-start.39 = (bf16[8,2,16,512]{3,2,1,0:T(8,128)(2,1)S(1)}, bf16[8,2,16,512]{3,2,1,0:T(8,128)(2,1)S(1)}, u32[]{:S(2)}, u32[]{:S(2)}) collective-permute-start(bf16[8,2,16,512]{3,2,1,0:T(8,128)(2,1)S(1)} %collective-permute-done.24.refs_12_), channel_id=1, source_target_pairs={{0,16},{16,0},{1,17},{17,1},{2,18},{18,2},{3,19},{19,3},{4,20},{20... | collective-permute-start | bytes 786440 | tf_op jit(solution)/shard_map/ppermute | solution.py:33
  77.4 20.1 %collective-permute-start.34 = (bf16[8,2,16,512]{3,2,1,0:T(8,128)(2,1)S(1)}, bf16[8,2,16,512]{3,2,1,0:T(8,128)(2,1)S(1)}, u32[]{:S(2)}, u32[]{:S(2)}) collective-permute-start(bf16[8,2,16,512]{3,2,1,0:T(8,128)(2,1)S(1)} %collective-permute-done.9.refs_5_), channel_id=1, source_target_pairs={{0,16},{16,0},{1,17},{17,1},{2,18},{18,2},{3,19},{19,3},{4,20},{20... | collective-permute-start | bytes 786440 | tf_op jit(solution)/shard_map/ppermute | solution.py:33
  78.9 20.9 %collective-permute-start.17 = (bf16[8,2,16,512]{3,2,1,0:T(8,128)(2,1)}, bf16[8,2,16,512]{3,2,1,0:T(8,128)(2,1)S(1)}, u32[]{:S(2)}, u32[]{:S(2)}) collective-permute-start(bf16[8,2,16,512]{3,2,1,0:T(8,128)(2,1)} %get-tuple-element.133), channel_id=1, source_target_pairs={{0,9},{1,8},{2,11},{3,10},{4,13},{5,12},{6,15},{7,14},{8,1},{9,0},... | collective-permute-start | bytes 786440 | tf_op jit(solution)/shard_map/ppermute | solution.py:33
  88.1 13.2 %collective-permute-start.45 = (bf16[8,2,16,512]{3,2,1,0:T(8,128)(2,1)S(1)}, bf16[8,2,16,512]{3,2,1,0:T(8,128)(2,1)S(1)}, u32[]{:S(2)}, u32[]{:S(2)}) collective-permute-start(bf16[8,2,16,512]{3,2,1,0:T(8,128)(2,1)S(1)} %collective-permute-done.16.refs_8_), channel_id=1, source_target_pairs={{0,16},{16,0},{1,17},{17,1},{2,18},{18,2},{3,19},{19,3},{4,20},{20... | collective-permute-start | bytes 786440 | tf_op jit(solution)/shard_map/ppermute | solution.py:33
  97.5 14.8 %collective-permute-start.40 = (bf16[8,2,16,512]{3,2,1,0:T(8,128)(2,1)S(1)}, bf16[8,2,16,512]{3,2,1,0:T(8,128)(2,1)S(1)}, u32[]{:S(2)}, u32[]{:S(2)}) collective-permute-start(bf16[8,2,16,512]{3,2,1,0:T(8,128)(2,1)S(1)} %collective-permute-done.25.refs_13_), channel_id=1, source_target_pairs={{0,16},{16,0},{1,17},{17,1},{2,18},{18,2},{3,19},{19,3},{4,20},{20... | collective-permute-start | bytes 786440 | tf_op jit(solution)/shard_map/ppermute | solution.py:33
  101.3 22.3 %collective-permute-start.18 = (bf16[8,2,16,512]{3,2,1,0:T(8,128)(2,1)}, bf16[8,2,16,512]{3,2,1,0:T(8,128)(2,1)S(1)}, u32[]{:S(2)}, u32[]{:S(2)}) collective-permute-start(bf16[8,2,16,512]{3,2,1,0:T(8,128)(2,1)} %get-tuple-element.134), channel_id=1, source_target_pairs={{0,10},{1,11},{2,8},{3,9},{4,14},{5,15},{6,12},{7,13},{8,2},{9,3},... | collective-permute-start | bytes 786440 | tf_op jit(solution)/shard_map/ppermute | solution.py:33
  106.3 18.0 %collective-permute-start.46 = (bf16[8,2,16,512]{3,2,1,0:T(8,128)(2,1)S(1)}, bf16[8,2,16,512]{3,2,1,0:T(8,128)(2,1)S(1)}, u32[]{:S(2)}, u32[]{:S(2)}) collective-permute-start(bf16[8,2,16,512]{3,2,1,0:T(8,128)(2,1)S(1)} %collective-permute-done.17.refs_9_), channel_id=1, source_target_pairs={{0,16},{16,0},{1,17},{17,1},{2,18},{18,2},{3,19},{19,3},{4,20},{20... | collective-permute-start | bytes 786440 | tf_op jit(solution)/shard_map/ppermute | solution.py:33
  108.7 15.7 %collective-permute-start.27 = (bf16[8,2,16,512]{3,2,1,0:T(8,128)(2,1)}, bf16[8,2,16,512]{3,2,1,0:T(8,128)(2,1)S(1)}, u32[]{:S(2)}, u32[]{:S(2)}) collective-permute-start(bf16[8,2,16,512]{3,2,1,0:T(8,128)(2,1)} %get-tuple-element.150), channel_id=1, source_target_pairs={{0,15},{1,14},{2,13},{3,12},{4,11},{5,10},{6,9},{7,8},{8,7},{9,6},... | collective-permute-start | bytes 786440 | tf_op jit(solution)/shard_map/ppermute | solution.py:33
  112.3 16.8 %collective-permute-start.6 = (bf16[8,2,16,512]{3,2,1,0:T(8,128)(2,1)}, bf16[8,2,16,512]{3,2,1,0:T(8,128)(2,1)S(1)}, u32[]{:S(2)}, u32[]{:S(2)}) collective-permute-start(bf16[8,2,16,512]{3,2,1,0:T(8,128)(2,1)} %get-tuple-element.109), channel_id=1, source_target_pairs={{0,2},{1,3},{2,0},{3,1},{4,6},{5,7},{6,4},{7,5},{8,10},{9,11},{10,... | collective-permute-start | bytes 786440 | tf_op jit(solution)/shard_map/ppermute | solution.py:33
  112.4 23.2 %collective-permute-start.41 = (bf16[8,2,16,512]{3,2,1,0:T(8,128)(2,1)S(1)}, bf16[8,2,16,512]{3,2,1,0:T(8,128)(2,1)S(1)}, u32[]{:S(2)}, u32[]{:S(2)}) collective-permute-start(bf16[8,2,16,512]{3,2,1,0:T(8,128)(2,1)S(1)} %collective-permute-done.26.refs_14_), channel_id=1, source_target_pairs={{0,16},{16,0},{1,17},{17,1},{2,18},{18,2},{3,19},{19,3},{4,20},{20... | collective-permute-start | bytes 786440 | tf_op jit(solution)/shard_map/ppermute | solution.py:33
  124.3 16.0 %collective-permute-start.19 = (bf16[8,2,16,512]{3,2,1,0:T(8,128)(2,1)}, bf16[8,2,16,512]{3,2,1,0:T(8,128)(2,1)S(1)}, u32[]{:S(2)}, u32[]{:S(2)}) collective-permute-start(bf16[8,2,16,512]{3,2,1,0:T(8,128)(2,1)} %get-tuple-element.135), channel_id=1, source_target_pairs={{0,11},{1,10},{2,9},{3,8},{4,15},{5,14},{6,13},{7,12},{8,3},{9,2},... | collective-permute-start | bytes 786440 | tf_op jit(solution)/shard_map/ppermute | solution.py:33
  124.3 16.3 %collective-permute-start.47 = (bf16[8,2,16,512]{3,2,1,0:T(8,128)(2,1)S(1)}, bf16[8,2,16,512]{3,2,1,0:T(8,128)(2,1)S(1)}, u32[]{:S(2)}, u32[]{:S(2)}) collective-permute-start(bf16[8,2,16,512]{3,2,1,0:T(8,128)(2,1)S(1)} %collective-permute-done.18.refs_10_), channel_id=1, source_target_pairs={{0,16},{16,0},{1,17},{17,1},{2,18},{18,2},{3,19},{19,3},{4,20},{20... | collective-permute-start | bytes 786440 | tf_op jit(solution)/shard_map/ppermute | solution.py:33
  129.1 16.0 %collective-permute-start.12 = (bf16[8,2,16,512]{3,2,1,0:T(8,128)(2,1)}, bf16[8,2,16,512]{3,2,1,0:T(8,128)(2,1)S(1)}, u32[]{:S(2)}, u32[]{:S(2)}) collective-permute-start(bf16[8,2,16,512]{3,2,1,0:T(8,128)(2,1)} %get-tuple-element.120), channel_id=1, source_target_pairs={{0,4},{1,5},{2,6},{3,7},{4,0},{5,1},{6,2},{7,3},{8,12},{9,13},{10,... | collective-permute-start | bytes 786440 | tf_op jit(solution)/shard_map/ppermute | solution.py:33
  140.7 15.6 %collective-permute-start.48 = (bf16[8,2,16,512]{3,2,1,0:T(8,128)(2,1)S(1)}, bf16[8,2,16,512]{3,2,1,0:T(8,128)(2,1)}, u32[]{:S(2)}, u32[]{:S(2)}) collective-permute-start(bf16[8,2,16,512]{3,2,1,0:T(8,128)(2,1)S(1)} %collective-permute-done.19.refs_11_), channel_id=1, source_target_pairs={{0,16},{16,0},{1,17},{17,1},{2,18},{18,2},{3,19},{19,3},{4,20},{20... | collective-permute-start | bytes 786440 | tf_op jit(solution)/shard_map/ppermute | solution.py:33
  146.8 17.1 %collective-permute-start.13 = (bf16[8,2,16,512]{3,2,1,0:T(8,128)(2,1)}, bf16[8,2,16,512]{3,2,1,0:T(8,128)(2,1)S(1)}, u32[]{:S(2)}, u32[]{:S(2)}) collective-permute-start(bf16[8,2,16,512]{3,2,1,0:T(8,128)(2,1)} %get-tuple-element.122), channel_id=1, source_target_pairs={{0,5},{1,4},{2,7},{3,6},{4,1},{5,0},{6,3},{7,2},{8,13},{9,12},{10,... | collective-permute-start | bytes 786440 | tf_op jit(solution)/shard_map/ppermute | solution.py:33
  146.9 29.1 %collective-permute-start.20 = (bf16[8,2,16,512]{3,2,1,0:T(8,128)(2,1)}, bf16[8,2,16,512]{3,2,1,0:T(8,128)(2,1)S(1)}, u32[]{:S(2)}, u32[]{:S(2)}) collective-permute-start(bf16[8,2,16,512]{3,2,1,0:T(8,128)(2,1)} %get-tuple-element.136), channel_id=1, source_target_pairs={{0,8},{1,9},{2,10},{3,11},{4,12},{5,13},{6,14},{7,15},{8,0},{9,1},... | collective-permute-start | bytes 786440 | tf_op jit(solution)/shard_map/ppermute | solution.py:33
  150.5 25.5 %collective-permute-start.43 = (bf16[8,2,16,512]{3,2,1,0:T(8,128)(2,1)S(1)}, bf16[8,2,16,512]{3,2,1,0:T(8,128)(2,1)S(1)}, u32[]{:S(2)}, u32[]{:S(2)}) collective-permute-start(bf16[8,2,16,512]{3,2,1,0:T(8,128)(2,1)S(1)} %collective-permute-done.5.refs_1_), channel_id=1, source_target_pairs={{0,16},{16,0},{1,17},{17,1},{2,18},{18,2},{3,19},{19,3},{4,20},{20... | collective-permute-start | bytes 786440 | tf_op jit(solution)/shard_map/ppermute | solution.py:33
  156.3 19.9 %collective-permute-start.50 = (bf16[8,2,16,512]{3,2,1,0:T(8,128)(2,1)S(1)}, bf16[8,2,16,512]{3,2,1,0:T(8,128)(2,1)S(1)}, u32[]{:S(2)}, u32[]{:S(2)}) collective-permute-start(bf16[8,2,16,512]{3,2,1,0:T(8,128)(2,1)S(1)} %collective-permute-done.7.refs_3_), channel_id=1, source_target_pairs={{0,16},{16,0},{1,17},{17,1},{2,18},{18,2},{3,19},{19,3},{4,20},{20... | collective-permute-start | bytes 786440 | tf_op jit(solution)/shard_map/ppermute | solution.py:33
  157.7 20.1 %collective-permute-start.49 = (bf16[8,2,16,512]{3,2,1,0:T(8,128)(2,1)S(1)}, bf16[8,2,16,512]{3,2,1,0:T(8,128)(2,1)S(1)}, u32[]{:S(2)}, u32[]{:S(2)}) collective-permute-start(bf16[8,2,16,512]{3,2,1,0:T(8,128)(2,1)S(1)} %collective-permute-done.6.refs_2_), channel_id=1, source_target_pairs={{0,16},{16,0},{1,17},{17,1},{2,18},{18,2},{3,19},{19,3},{4,20},{20... | collective-permute-start | bytes 786440 | tf_op jit(solution)/shard_map/ppermute | solution.py:33
  163.9 14.3 %collective-permute-start.29 = (bf16[8,2,16,512]{3,2,1,0:T(8,128)(2,1)}, bf16[8,2,16,512]{3,2,1,0:T(8,128)(2,1)S(1)}, u32[]{:S(2)}, u32[]{:S(2)}) collective-permute-start(bf16[8,2,16,512]{3,2,1,0:T(8,128)(2,1)} %get-tuple-element.153), channel_id=1, source_target_pairs={{0,13},{1,12},{2,15},{3,14},{4,9},{5,8},{6,11},{7,10},{8,5},{9,4},... | collective-permute-start | bytes 786440 | tf_op jit(solution)/shard_map/ppermute | solution.py:33
  176.0 21.1 %collective-permute-start.21 = (bf16[8,2,16,512]{3,2,1,0:T(8,128)(2,1)}, bf16[8,2,16,512]{3,2,1,0:T(8,128)(2,1)S(1)}, u32[]{:S(2)}, u32[]{:S(2)}) collective-permute-start(bf16[8,2,16,512]{3,2,1,0:T(8,128)(2,1)} %get-tuple-element.138), channel_id=1, source_target_pairs={{0,9},{1,8},{2,11},{3,10},{4,13},{5,12},{6,15},{7,14},{8,1},{9,0},... | collective-permute-start | bytes 786440 | tf_op jit(solution)/shard_map/ppermute | solution.py:33
  176.1 21.0 %collective-permute-start.51 = (bf16[8,2,16,512]{3,2,1,0:T(8,128)(2,1)S(1)}, bf16[8,2,16,512]{3,2,1,0:T(8,128)(2,1)}, u32[]{:S(2)}, u32[]{:S(2)}) collective-permute-start(bf16[8,2,16,512]{3,2,1,0:T(8,128)(2,1)S(1)} %collective-permute-done.12.refs_4_), channel_id=1, source_target_pairs={{0,16},{16,0},{1,17},{17,1},{2,18},{18,2},{3,19},{19,3},{4,20},{20... | collective-permute-start | bytes 786440 | tf_op jit(solution)/shard_map/ppermute | solution.py:33
  177.9 23.0 %collective-permute-start.55 = (bf16[8,2,16,512]{3,2,1,0:T(8,128)(2,1)S(1)}, bf16[8,2,16,512]{3,2,1,0:T(8,128)(2,1)}, u32[]{:S(2)}, u32[]{:S(2)}) collective-permute-start(bf16[8,2,16,512]{3,2,1,0:T(8,128)(2,1)S(1)} %collective-permute-done.20.refs_8_), channel_id=1, source_target_pairs={{0,16},{16,0},{1,17},{17,1},{2,18},{18,2},{3,19},{19,3},{4,20},{20... | collective-permute-start | bytes 786440 | tf_op jit(solution)/shard_map/ppermute | solution.py:33
  178.3 23.3 %collective-permute-start.59 = (bf16[8,2,16,512]{3,2,1,0:T(8,128)(2,1)S(1)}, bf16[8,2,16,512]{3,2,1,0:T(8,128)(2,1)}, u32[]{:S(2)}, u32[]{:S(2)}) collective-permute-start(bf16[8,2,16,512]{3,2,1,0:T(8,128)(2,1)S(1)} %collective-permute-done.28.refs_12_), channel_id=1, source_target_pairs={{0,16},{16,0},{1,17},{17,1},{2,18},{18,2},{3,19},{19,3},{4,20},{20... | collective-permute-start | bytes 786440 | tf_op jit(solution)/shard_map/ppermute | solution.py:33
  184.8 18.1 %collective-permute-start.30 = (bf16[8,2,16,512]{3,2,1,0:T(8,128)(2,1)}, bf16[8,2,16,512]{3,2,1,0:T(8,128)(2,1)S(1)}, u32[]{:S(2)}, u32[]{:S(2)}) collective-permute-start(bf16[8,2,16,512]{3,2,1,0:T(8,128)(2,1)} %get-tuple-element.155), channel_id=1, source_target_pairs={{0,14},{1,15},{2,12},{3,13},{4,10},{5,11},{6,8},{7,9},{8,6},{9,7},... | collective-permute-start | bytes 786440 | tf_op jit(solution)/shard_map/ppermute | solution.py:33
  197.2 26.4 %collective-permute-start.15 = (bf16[8,2,16,512]{3,2,1,0:T(8,128)(2,1)}, bf16[8,2,16,512]{3,2,1,0:T(8,128)(2,1)S(1)}, u32[]{:S(2)}, u32[]{:S(2)}) collective-permute-start(bf16[8,2,16,512]{3,2,1,0:T(8,128)(2,1)} %get-tuple-element.126), channel_id=1, source_target_pairs={{0,7},{1,6},{2,5},{3,4},{4,3},{5,2},{6,1},{7,0},{8,15},{9,14},{10,... | collective-permute-start | bytes 786440 | tf_op jit(solution)/shard_map/ppermute | solution.py:33
  197.2 19.6 %collective-permute-start.22 = (bf16[8,2,16,512]{3,2,1,0:T(8,128)(2,1)}, bf16[8,2,16,512]{3,2,1,0:T(8,128)(2,1)S(1)}, u32[]{:S(2)}, u32[]{:S(2)}) collective-permute-start(bf16[8,2,16,512]{3,2,1,0:T(8,128)(2,1)} %get-tuple-element.140), channel_id=1, source_target_pairs={{0,10},{1,11},{2,8},{3,9},{4,14},{5,15},{6,12},{7,13},{8,2},{9,3},... | collective-permute-start | bytes 786440 | tf_op jit(solution)/shard_map/ppermute | solution.py:33
  200.9 17.0 %collective-permute-start.52 = (bf16[8,2,16,512]{3,2,1,0:T(8,128)(2,1)S(1)}, bf16[8,2,16,512]{3,2,1,0:T(8,128)(2,1)S(1)}, u32[]{:S(2)}, u32[]{:S(2)}) collective-permute-start(bf16[8,2,16,512]{3,2,1,0:T(8,128)(2,1)S(1)} %collective-permute-done.13.refs_5_), channel_id=1, source_target_pairs={{0,16},{16,0},{1,17},{17,1},{2,18},{18,2},{3,19},{19,3},{4,20},{20... | collective-permute-start | bytes 786440 | tf_op jit(solution)/shard_map/ppermute | solution.py:33
  201.5 20.0 %collective-permute-start.56 = (bf16[8,2,16,512]{3,2,1,0:T(8,128)(2,1)S(1)}, bf16[8,2,16,512]{3,2,1,0:T(8,128)(2,1)S(1)}, u32[]{:S(2)}, u32[]{:S(2)}) collective-permute-start(bf16[8,2,16,512]{3,2,1,0:T(8,128)(2,1)S(1)} %collective-permute-done.21.refs_9_), channel_id=1, source_target_pairs={{0,16},{16,0},{1,17},{17,1},{2,18},{18,2},{3,19},{19,3},{4,20},{20... | collective-permute-start | bytes 786440 | tf_op jit(solution)/shard_map/ppermute | solution.py:33
  202.9 20.1 %collective-permute-start.60 = (bf16[8,2,16,512]{3,2,1,0:T(8,128)(2,1)S(1)}, bf16[8,2,16,512]{3,2,1,0:T(8,128)(2,1)S(1)}, u32[]{:S(2)}, u32[]{:S(2)}) collective-permute-start(bf16[8,2,16,512]{3,2,1,0:T(8,128)(2,1)S(1)} %collective-permute-done.29.refs_13_), channel_id=1, source_target_pairs={{0,16},{16,0},{1,17},{17,1},{2,18},{18,2},{3,19},{19,3},{4,20},{20... | collective-permute-start | bytes 786440 | tf_op jit(solution)/shard_map/ppermute | solution.py:33
  216.8 28.9 %collective-permute-start.31 = (bf16[8,2,16,512]{3,2,1,0:T(8,128)(2,1)}, bf16[8,2,16,512]{3,2,1,0:T(8,128)(2,1)S(1)}, u32[]{:S(2)}, u32[]{:S(2)}) collective-permute-start(bf16[8,2,16,512]{3,2,1,0:T(8,128)(2,1)} %get-tuple-element.157), channel_id=1, source_target_pairs={{0,15},{1,14},{2,13},{3,12},{4,11},{5,10},{6,9},{7,8},{8,7},{9,6},... | collective-permute-start | bytes 786440 | tf_op jit(solution)/shard_map/ppermute | solution.py:33
  217.9 26.5 %collective-permute-start.23 = (bf16[8,2,16,512]{3,2,1,0:T(8,128)(2,1)}, bf16[8,2,16,512]{3,2,1,0:T(8,128)(2,1)S(1)}, u32[]{:S(2)}, u32[]{:S(2)}) collective-permute-start(bf16[8,2,16,512]{3,2,1,0:T(8,128)(2,1)} %get-tuple-element.142), channel_id=1, source_target_pairs={{0,11},{1,10},{2,9},{3,8},{4,15},{5,14},{6,13},{7,12},{8,3},{9,2},... | collective-permute-start | bytes 786440 | tf_op jit(solution)/shard_map/ppermute | solution.py:33
  221.6 16.4 %collective-permute-start.53 = (bf16[8,2,16,512]{3,2,1,0:T(8,128)(2,1)S(1)}, bf16[8,2,16,512]{3,2,1,0:T(8,128)(2,1)S(1)}, u32[]{:S(2)}, u32[]{:S(2)}) collective-permute-start(bf16[8,2,16,512]{3,2,1,0:T(8,128)(2,1)S(1)} %collective-permute-done.14.refs_6_), channel_id=1, source_target_pairs={{0,16},{16,0},{1,17},{17,1},{2,18},{18,2},{3,19},{19,3},{4,20},{20... | collective-permute-start | bytes 786440 | tf_op jit(solution)/shard_map/ppermute | solution.py:33
  223.0 21.4 %collective-permute-start.57 = (bf16[8,2,16,512]{3,2,1,0:T(8,128)(2,1)S(1)}, bf16[8,2,16,512]{3,2,1,0:T(8,128)(2,1)S(1)}, u32[]{:S(2)}, u32[]{:S(2)}) collective-permute-start(bf16[8,2,16,512]{3,2,1,0:T(8,128)(2,1)S(1)} %collective-permute-done.22.refs_10_), channel_id=1, source_target_pairs={{0,16},{16,0},{1,17},{17,1},{2,18},{18,2},{3,19},{19,3},{4,20},{20... | collective-permute-start | bytes 786440 | tf_op jit(solution)/shard_map/ppermute | solution.py:33
  223.6 22.1 %collective-permute-start.61 = (bf16[8,2,16,512]{3,2,1,0:T(8,128)(2,1)S(1)}, bf16[8,2,16,512]{3,2,1,0:T(8,128)(2,1)S(1)}, u32[]{:S(2)}, u32[]{:S(2)}) collective-permute-start(bf16[8,2,16,512]{3,2,1,0:T(8,128)(2,1)S(1)} %collective-permute-done.30.refs_14_), channel_id=1, source_target_pairs={{0,16},{16,0},{1,17},{17,1},{2,18},{18,2},{3,19},{19,3},{4,20},{20... | collective-permute-start | bytes 786440 | tf_op jit(solution)/shard_map/ppermute | solution.py:33
  238.0 20.0 %collective-permute-start.54 = (bf16[8,2,16,512]{3,2,1,0:T(8,128)(2,1)S(1)}, bf16[8,2,16,512]{3,2,1,0:T(8,128)(2,1)S(1)}, u32[]{:S(2)}, u32[]{:S(2)}) collective-permute-start(bf16[8,2,16,512]{3,2,1,0:T(8,128)(2,1)S(1)} %collective-permute-done.15.refs_7_), channel_id=1, source_target_pairs={{0,16},{16,0},{1,17},{17,1},{2,18},{18,2},{3,19},{19,3},{4,20},{20... | collective-permute-start | bytes 786440 | tf_op jit(solution)/shard_map/ppermute | solution.py:33
  244.4 13.6 %collective-permute-start.58 = (bf16[8,2,16,512]{3,2,1,0:T(8,128)(2,1)S(1)}, bf16[8,2,16,512]{3,2,1,0:T(8,128)(2,1)S(1)}, u32[]{:S(2)}, u32[]{:S(2)}) collective-permute-start(bf16[8,2,16,512]{3,2,1,0:T(8,128)(2,1)S(1)} %collective-permute-done.23.refs_11_), channel_id=1, source_target_pairs={{0,16},{16,0},{1,17},{17,1},{2,18},{18,2},{3,19},{19,3},{4,20},{20... | collective-permute-start | bytes 786440 | tf_op jit(solution)/shard_map/ppermute | solution.py:33
  (74 other events, 3651.3 us)

commit v3 on v2

--- a/solution.py
+++ b/solution.py
@@ -11,9 +11,6 @@
 
 VMEM_LIMIT = 56 << 20
 HALVES = 2
-CUT = 1
-OWN_AT = 1
-OTHER_AT = 4
 FIRST = 2
 XLAG = 3
 ZORD = (1, 3, 2)
@@ -178,58 +175,64 @@
     return dict(enumerate(outs))
 
 
-def correlate_body(count, n, crossed, group_ref, *refs):
-    out_ref, token_ref = refs[-2:]
-    frames, inputs = refs[0].shape[2:]
-
-    def parts(pieces):
-        return [
-            jnp.concatenate([piece[0, r] for piece in pieces], axis=0) for r in range(2)
-        ]
-
-    own = parts(refs[:n])
-    real, imag = parts(refs[n : 2 * n]) if crossed else own
-    rows = jnp.transpose(jnp.concatenate(own, axis=0))
+def stacked(pieces):
+    return [jnp.concatenate([piece[0, r] for piece in pieces], axis=0) for r in range(2)]
+
+
+def products(count, rows, real, imag, out_ref):
     for which, pair in enumerate(((real, imag), (imag, -real))):
         product = jnp.dot(rows, jnp.concatenate(pair, axis=0), preferred_element_type=jnp.float32)
         out_ref[0, which] = product * (1.0 / count)
-    token_ref[...] = jnp.zeros_like(token_ref)
-
-
-def correlate(group, own, other, earlier, shape, first, start, channels, count):
-    n = len(own)
-    _, _, frames, inputs = own[0].shape
-    pieces = own + (other or [])
+
+
+def own_body(count, n, group_ref, *refs):
+    out_ref, rows_ref = refs[-2:]
+    real, imag = stacked(refs[:n])
+    rows = jnp.transpose(jnp.concatenate([real, imag], axis=0))
+    rows_ref[0] = rows
+    products(count, rows, real, imag, out_ref)
+
+
+def other_body(count, n, group_ref, rows_ref, *refs):
+    real, imag = stacked(refs[:n])
+    products(count, rows_ref[0], real, imag, refs[-1])
+
+
+def correlate(group, rows, pieces, earlier, shape, first, count):
+    n = len(pieces)
+    channels, _, frames, inputs = pieces[0].shape
+    depth = 2 * n * frames
+    crossed = rows is not None
+    before = [rows] if crossed else []
     held = [] if earlier is None else [earlier]
-    crossed = other is not None
-    spec = pl.BlockSpec((1, 2, frames, inputs), lambda c, g: (start + c, 0, 0, 0))
-    return pl.pallas_call(
-        functools.partial(correlate_body, count, n, crossed),
+    spec = pl.BlockSpec((1, 2, frames, inputs), lambda c, g: (c, 0, 0, 0))
+    rows_spec = pl.BlockSpec((1, inputs, depth), lambda c, g: (c, 0, 0))
+    out_spec = pl.BlockSpec(
+        (1, 2, inputs, inputs), lambda c, g: (first + c, 0, 0, 1 - g[0] if crossed else g[0])
+    )
+    out_shape = jax.ShapeDtypeStruct(shape, jnp.float32)
+    rows_shape = jax.ShapeDtypeStruct((channels, inputs, depth), jnp.bfloat16)
+    outs = pl.pallas_call(
+        functools.partial(other_body if crossed else own_body, count, n),
         grid_spec=pltpu.PrefetchScalarGridSpec(
             num_scalar_prefetch=1,
             grid=(channels,),
-            in_specs=[spec] * len(pieces) + [pl.BlockSpec(memory_space=pl.ANY)] * len(held),
-            out_specs=[
-                pl.BlockSpec(
-                    (1, 2, inputs, inputs),
-                    lambda c, g: (first + start + c, 0, 0, 1 - g[0] if crossed else g[0]),
-                ),
-                pl.BlockSpec((8, 128), lambda c, g: (0, 0)),
-            ],
-        ),
-        out_shape=[
-            jax.ShapeDtypeStruct(shape, jnp.float32),
-            jax.ShapeDtypeStruct((8, 128), jnp.float32),
-        ],
-        input_output_aliases={1 + len(pieces): 0} if held else {},
+            in_specs=[rows_spec] * len(before)
+            + [spec] * n
+            + [pl.BlockSpec(memory_space=pl.ANY)] * len(held),
+            out_specs=[out_spec] if crossed else [out_spec, rows_spec],
+        ),
+        out_shape=[out_shape] if crossed else [out_shape, rows_shape],
+        input_output_aliases={1 + len(before) + n: 0} if held else {},
         compiler_params=pltpu.CompilerParams(vmem_limit_bytes=VMEM_LIMIT),
         cost_estimate=pl.CostEstimate(
-            flops=channels * 8 * inputs * inputs * n * frames,
-            bytes_accessed=channels * 4 * inputs * (2 * inputs + 2 * n * frames),
+            flops=channels * 4 * inputs * inputs * depth,
+            bytes_accessed=channels * 4 * inputs * (2 * inputs + depth),
             transcendentals=0,
         ),
         name="correlate_other" if crossed else "correlate_own",
-    )(group, *pieces, *held)
+    )(group, *before, *pieces, *held)
+    return outs[0], rows if crossed else outs[1]
 
 
 def turn_orders(devices):
@@ -255,7 +258,7 @@
     shape = (own_channels, 2, inputs, inputs * lax.axis_size("inp"))
 
     far, close, order = turn_orders(devices)
-    come, others, tokens = {}, {}, []
+    come, others = {}, {}
     far_chain, close_chain, chain = [], [], []
     result = None
 
@@ -278,18 +281,11 @@
         for k, d in enumerate(order):
             if (h, d) in others:
                 continue
-            more = [token for at, token in zip((OWN_AT, OTHER_AT), tokens) if at == k]
-            send((h, d), come[h, d], chain, XLAG, "inp", 1, others, more)
+            send((h, d), come[h, d], chain, XLAG, "inp", 1, others)
         own = [come[h, d] for d in range(devices)]
         other = [others[h, d] for d in range(devices)]
-        tokens = []
-        cut = max(1, part // CUT)
-        for crossed in (None, other):
-            for start in range(0, part, cut):
-                result, token = correlate(
-                    group, own, crossed, result, shape, h * part, start, min(cut, part - start), count
-                )
-                tokens.append(token)
+        result, rows = correlate(group, None, own, result, shape, h * part, count)
+        result, _ = correlate(group, rows, other, result, shape, h * part, count)
     return result
 
 

time: 276 us -> 272 us (0.986)
  waiting for transfers between devices: 93 us -> 90.2 us
    ppermute x62, waiting for transfers between devices: 93 us -> 90.2 us  [from_partner(): lax.ppermute(value, axis, [(i, i ^ by) for i in range(lax.axis_size(axis))])]
  transfers between devices with their start and end apart: 63 -> 63, of which waited for: 22 -> 23; matrix products, arithmetic and copies ran while one was open for 0% -> 0% of each run, Pallas kernels for 20% -> 20%
where the time goes in v3:
time: 272 us; the launch traced here: 270 us
  starting transfers between devices  103 us (38%)
  waiting for transfers between devices  90.2 us (33%)
  Pallas kernels  71.4 us (26%)
  local copies, waits for them, and re-layouts  4.3 us (2%)
    ppermute x62, starting transfers between devices, from_partner(): lax.ppermute(value, axis, [(i, i ^ by) for i in range(lax.axis_size(axis))])  101 us
    ppermute x62, waiting for transfers between devices, from_partner(): lax.ppermute(value, axis, [(i, i ^ by) for i in range(lax.axis_size(axis))])  90.2 us
    pallas_call x4, Pallas kernels, correlate(): pl.pallas_call(functools.partial(other_body if crossed else own_body, cou...  47.6 us
    pallas_call x2, Pallas kernels, make_pieces(): pl.pallas_call(functools.partial(pieces_body, group), grid_spec=pltpu.Pre...  12.4 us
    pallas_call x1, Pallas kernels, late_spectra(): pl.pallas_call(late_body, grid_spec=pltpu.PrefetchScalarGridSpec(num_scal...  11.4 us
  transfers between devices with their start and end apart: 63, of which 23 were waited for; matrix products, arithmetic and copies ran while one was open for 0% of the time, Pallas kernels for 20%

profile of v3, /device:TPU:0, one launch (start us, length us, event | category | flops | bytes accessed | tf_op | source)
XLA Modules:
  0.0 269.9 jit_solution(7583680723909366736)
XLA Ops:
  1.5 2.5 collective-permute-start
  4.0 11.4 %late_spectra.1.late_ref = bf16[13,512,512]{2,1,0:T(8,128)(2,1)} custom-call(s32[1]{0:T(128)} %bitcast.1.here_ref, f32[4,512]{1,0:T(4,128)} %taps_ref.5, bf16[2,16,16,512]{3,2,1,0:T(8,128)(2,1)} %constant.13.clone.table_ref, bf16[512,8192]{1,0:T(8,128)(2,1)} %raw_ref.5), custom_call_target="tpu_custom_call" | custom-call | flops 4294967296 | bytes 16777216 | tf_op jit(solution)/shard_map/late_spectra/pallas_call | solution.py:114
  16.5 6.2 %pieces.2 = (bf16[8,2,16,512]{3,2,1,0:T(8,128)(2,1)}, bf16[8,2,16,512]{3,2,1,0:T(8,128)(2,1)}, bf16[8,2,16,512]{3,2,1,0:T(8,128)(2,1)}, bf16[8,2,16,512]{3,2,1,0...) custom-call(s32[1]{0:T(128)} %bitcast.1.here_ref, ...), custom_call_target="tpu_custom_call" | custom-call | flops 1073741824 | bytes 8388608 | tf_op jit(solution)/shard_map/pieces/pallas_call | solution.py:148
  22.7 8.5 %collective-permute-start.2 = (bf16[8,2,16,512]{3,2,1,0:T(8,128)(2,1)}, bf16[8,2,16,512]{3,2,1,0:T(8,128)(2,1)S(1)}, u32[]{:S(2)}, u32[]{:S(2)}) collective-permute-start(bf16[8,2,16,512]{3,2,1,0:T(8,128)(2,1)} %get-tuple-element.104), channel_id=1, source_target_pairs={{0,1},{1,0},{2,3},{3,2},{4,5},{5,4},{6,7},{7,6},{8,9},{9,8},{10,11... | collective-permute-start | bytes 786440 | tf_op jit(solution)/shard_map/ppermute | solution.py:30
  32.6 2.7 %collective-permute-start.3 = (bf16[8,2,16,512]{3,2,1,0:T(8,128)(2,1)}, bf16[8,2,16,512]{3,2,1,0:T(8,128)(2,1)S(1)}, u32[]{:S(2)}, u32[]{:S(2)}) collective-permute-start(bf16[8,2,16,512]{3,2,1,0:T(8,128)(2,1)} %get-tuple-element.105), channel_id=1, source_target_pairs={{0,2},{1,3},{2,0},{3,1},{4,6},{5,7},{6,4},{7,5},{8,10},{9,11},{10,... | collective-permute-start | bytes 786440 | tf_op jit(solution)/shard_map/ppermute | solution.py:30
  35.4 1.6 collective-permute-start.8
  39.0 2.5 collective-permute-start.24
  46.4 2.6 collective-permute-start.16
  49.0 1.6 collective-permute-done.32.refs_1_
  54.5 7.4 %collective-permute-done.9.refs_5_ = bf16[8,2,16,512]{3,2,1,0:T(8,128)(2,1)S(1)} collective-permute-done((bf16[8,2,16,512]{3,2,1,0:T(8,128)(2,1)}, bf16[8,2,16,512]{3,2,1,0:T(8,128)(2,1)S(1)}, u32[]{:S(2)}, u32[]{:S(2)}) %collective-permute-start.9) | collective-permute-done | bytes 262176 | tf_op jit(solution)/shard_map/ppermute | solution.py:30
  63.4 5.4 %collective-permute-done.16.refs_8_ = bf16[8,2,16,512]{3,2,1,0:T(8,128)(2,1)S(1)} collective-permute-done((bf16[8,2,16,512]{3,2,1,0:T(8,128)(2,1)}, bf16[8,2,16,512]{3,2,1,0:T(8,128)(2,1)S(1)}, u32[]{:S(2)}, u32[]{:S(2)}) %collective-permute-start.16) | collective-permute-done | bytes 262176 | tf_op jit(solution)/shard_map/ppermute | solution.py:30
  68.9 3.5 %collective-permute-start.10 = (bf16[8,2,16,512]{3,2,1,0:T(8,128)(2,1)}, bf16[8,2,16,512]{3,2,1,0:T(8,128)(2,1)S(1)}, u32[]{:S(2)}, u32[]{:S(2)}) collective-permute-start(bf16[8,2,16,512]{3,2,1,0:T(8,128)(2,1)} %get-tuple-element.118), channel_id=1, source_target_pairs={{0,6},{1,7},{2,4},{3,5},{4,2},{5,3},{6,0},{7,1},{8,14},{9,15},{10,... | collective-permute-start | bytes 786440 | tf_op jit(solution)/shard_map/ppermute | solution.py:30
  72.4 1.6 collective-permute-start.43
  74.6 2.9 %collective-permute-start.26 = (bf16[8,2,16,512]{3,2,1,0:T(8,128)(2,1)}, bf16[8,2,16,512]{3,2,1,0:T(8,128)(2,1)S(1)}, u32[]{:S(2)}, u32[]{:S(2)}) collective-permute-start(bf16[8,2,16,512]{3,2,1,0:T(8,128)(2,1)} %get-tuple-element.149), channel_id=1, source_target_pairs={{0,14},{1,15},{2,12},{3,13},{4,10},{5,11},{6,8},{7,9},{8,6},{9,7},... | collective-permute-start | bytes 786440 | tf_op jit(solution)/shard_map/ppermute | solution.py:30
  77.5 5.2 %collective-permute-done.10.refs_6_ = bf16[8,2,16,512]{3,2,1,0:T(8,128)(2,1)S(1)} collective-permute-done((bf16[8,2,16,512]{3,2,1,0:T(8,128)(2,1)}, bf16[8,2,16,512]{3,2,1,0:T(8,128)(2,1)S(1)}, u32[]{:S(2)}, u32[]{:S(2)}) %collective-permute-start.10) | collective-permute-done | bytes 262176 | tf_op jit(solution)/shard_map/ppermute | solution.py:30
  84.1 6.2 %pieces.3 = (bf16[8,2,16,512]{3,2,1,0:T(8,128)(2,1)}, bf16[8,2,16,512]{3,2,1,0:T(8,128)(2,1)}, bf16[8,2,16,512]{3,2,1,0:T(8,128)(2,1)}, bf16[8,2,16,512]{3,2,1,0...) custom-call(s32[1]{0:T(128)} %bitcast.1.here_ref, ...), custom_call_target="tpu_custom_call" | custom-call | flops 1073741824 | bytes 8388608 | tf_op jit(solution)/shard_map/pieces/pallas_call | solution.py:148
  90.4 2.4 collective-permute-done.17.refs_9_
  93.7 1.6 collective-permute-start.44
  95.9 7.5 %collective-permute-start.18 = (bf16[8,2,16,512]{3,2,1,0:T(8,128)(2,1)S(1)}, bf16[8,2,16,512]{3,2,1,0:T(8,128)(2,1)S(1)}, u32[]{:S(2)}, u32[]{:S(2)}) collective-permute-start(bf16[8,2,16,512]{3,2,1,0:T(8,128)(2,1)S(1)} %copy-done.59), channel_id=1, source_target_pairs={{0,10},{1,11},{2,8},{3,9},{4,14},{5,15},{6,12},{7,13},{8,2},{9,3},... | collective-permute-start | bytes 786440 | tf_op jit(solution)/shard_map/ppermute | solution.py:30
  106.9 1.7 collective-permute-done.37.refs_6_
  110.0 11.7 %collective-permute-done.18.refs_10_ = bf16[8,2,16,512]{3,2,1,0:T(8,128)(2,1)S(1)} collective-permute-done((bf16[8,2,16,512]{3,2,1,0:T(8,128)(2,1)S(1)}, bf16[8,2,16,512]{3,2,1,0:T(8,128)(2,1)S(1)}, u32[]{:S(2)}, u32[]{:S(2)}) %collective-permute-start.18) | collective-permute-done | bytes 262176 | tf_op jit(solution)/shard_map/ppermute | solution.py:30
  122.4 1.6 collective-permute-start.41
  123.9 9.3 %collective-permute-start.12 = (bf16[8,2,16,512]{3,2,1,0:T(8,128)(2,1)}, bf16[8,2,16,512]{3,2,1,0:T(8,128)(2,1)S(1)}, u32[]{:S(2)}, u32[]{:S(2)}) collective-permute-start(bf16[8,2,16,512]{3,2,1,0:T(8,128)(2,1)} %get-tuple-element.120), channel_id=1, source_target_pairs={{0,4},{1,5},{2,6},{3,7},{4,0},{5,1},{6,2},{7,3},{8,12},{9,13},{10,... | collective-permute-start | bytes 786440 | tf_op jit(solution)/shard_map/ppermute | solution.py:30
  134.2 1.7 collective-permute-start.46
  135.8 2.6 collective-permute-done.19.refs_11_
  140.5 3.5 %collective-permute-done.12.refs_4_ = bf16[8,2,16,512]{3,2,1,0:T(8,128)(2,1)S(1)} collective-permute-done((bf16[8,2,16,512]{3,2,1,0:T(8,128)(2,1)}, bf16[8,2,16,512]{3,2,1,0:T(8,128)(2,1)S(1)}, u32[]{:S(2)}, u32[]{:S(2)}) %collective-permute-start.12) | collective-permute-done | bytes 262176 | tf_op jit(solution)/shard_map/ppermute | solution.py:30
  145.0 2.8 %collective-permute-start.20 = (bf16[8,2,16,512]{3,2,1,0:T(8,128)(2,1)}, bf16[8,2,16,512]{3,2,1,0:T(8,128)(2,1)}, u32[]{:S(2)}, u32[]{:S(2)}) collective-permute-start(bf16[8,2,16,512]{3,2,1,0:T(8,128)(2,1)} %get-tuple-element.136), channel_id=1, source_target_pairs={{0,8},{1,9},{2,10},{3,11},{4,12},{5,13},{6,14},{7,15},{8,0},{9,1},... | collective-permute-start | bytes 786440 | tf_op jit(solution)/shard_map/ppermute | solution.py:30
  149.0 1.7 collective-permute-start.48
  150.6 4.1 %collective-permute-done.42.refs_11_ = bf16[8,2,16,512]{3,2,1,0:T(8,128)(2,1)} collective-permute-done((bf16[8,2,16,512]{3,2,1,0:T(8,128)(2,1)S(1)}, bf16[8,2,16,512]{3,2,1,0:T(8,128)(2,1)}, u32[]{:S(2)}, u32[]{:S(2)}) %collective-permute-start.42) | collective-permute-done | bytes 262176 | tf_op jit(solution)/shard_map/ppermute | solution.py:30
  154.7 1.7 collective-permute-start.50
  156.7 5.3 %collective-permute-done.13.refs_5_ = bf16[8,2,16,512]{3,2,1,0:T(8,128)(2,1)S(1)} collective-permute-done((bf16[8,2,16,512]{3,2,1,0:T(8,128)(2,1)}, bf16[8,2,16,512]{3,2,1,0:T(8,128)(2,1)S(1)}, u32[]{:S(2)}, u32[]{:S(2)}) %collective-permute-start.13) | collective-permute-done | bytes 262176 | tf_op jit(solution)/shard_map/ppermute | solution.py:30
  162.1 1.5 collective-permute-start.29
  163.6 11.5 %collective-permute-done.20.refs_8_ = bf16[8,2,16,512]{3,2,1,0:T(8,128)(2,1)} collective-permute-done((bf16[8,2,16,512]{3,2,1,0:T(8,128)(2,1)}, bf16[8,2,16,512]{3,2,1,0:T(8,128)(2,1)}, u32[]{:S(2)}, u32[]{:S(2)}) %collective-permute-start.20) | collective-permute-done | bytes 262176 | tf_op jit(solution)/shard_map/ppermute | solution.py:30
  178.8 5.8 %collective-permute-done.14.refs_6_ = bf16[8,2,16,512]{3,2,1,0:T(8,128)(2,1)S(1)} collective-permute-done((bf16[8,2,16,512]{3,2,1,0:T(8,128)(2,1)}, bf16[8,2,16,512]{3,2,1,0:T(8,128)(2,1)S(1)}, u32[]{:S(2)}, u32[]{:S(2)}) %collective-permute-start.14) | collective-permute-done | bytes 262176 | tf_op jit(solution)/shard_map/ppermute | solution.py:30
  185.4 2.5 collective-permute-start.30
  187.8 8.4 %collective-permute-done.21.refs_9_ = bf16[8,2,16,512]{3,2,1,0:T(8,128)(2,1)} collective-permute-done((bf16[8,2,16,512]{3,2,1,0:T(8,128)(2,1)}, bf16[8,2,16,512]{3,2,1,0:T(8,128)(2,1)}, u32[]{:S(2)}, u32[]{:S(2)}) %collective-permute-start.21) | collective-permute-done | bytes 262176 | tf_op jit(solution)/shard_map/ppermute | solution.py:30
  196.3 3.1 %collective-permute-start.22 = (bf16[8,2,16,512]{3,2,1,0:T(8,128)(2,1)}, bf16[8,2,16,512]{3,2,1,0:T(8,128)(2,1)S(1)}, u32[]{:S(2)}, u32[]{:S(2)}) collective-permute-start(bf16[8,2,16,512]{3,2,1,0:T(8,128)(2,1)} %get-tuple-element.140), channel_id=1, source_target_pairs={{0,10},{1,11},{2,8},{3,9},{4,14},{5,15},{6,12},{7,13},{8,2},{9,3},... | collective-permute-start | bytes 786440 | tf_op jit(solution)/shard_map/ppermute | solution.py:30
  199.4 1.6 collective-permute-start.52
  201.4 1.6 collective-permute-start.60
  203.1 11.2 %correlate_own.2 = (f32[16,2,512,1024]{3,2,1,0:T(8,128)}, bf16[8,512,512]{2,1,0:T(8,128)(2,1)}) custom-call(s32[1]{0:T(128)} %bitcast.group_ref, bf16[8,2,16,512]{3,2,1,0:T(8,128)(2,1)} %get-tuple-element.98.refs_0_, bf16[8,2,16,512]{3,2,1,0:T(8,128)(2,1)} %copy-done.41, bf16[8,2,16,512]{3,2,1,0:T(8,128)(2,1)} %copy-done.42, ...), custom_call_target="tpu_custom_call" | custom-call | flops 4294967296 | bytes 25165824 | tf_op jit(solution)/shard_map/correlate_own/pallas_call | solution.py:215
  215.2 4.0 %collective-permute-start.23 = (bf16[8,2,16,512]{3,2,1,0:T(8,128)(2,1)S(1)}, bf16[8,2,16,512]{3,2,1,0:T(8,128)(2,1)S(1)}, u32[]{:S(2)}, u32[]{:S(2)}) collective-permute-start(bf16[8,2,16,512]{3,2,1,0:T(8,128)(2,1)S(1)} %copy-done.49), channel_id=1, source_target_pairs={{0,11},{1,10},{2,9},{3,8},{4,15},{5,14},{6,13},{7,12},{8,3},{9,2},... | collective-permute-start | bytes 786440 | tf_op jit(solution)/shard_map/ppermute | solution.py:30
  219.2 2.1 collective-permute-start.53
  221.4 1.9 collective-permute-start.61
  223.4 12.6 %correlate_other.2.refs_16_ = f32[16,2,512,1024]{3,2,1,0:T(8,128)} custom-call(s32[1]{0:T(128)} %bitcast.group_ref, bf16[8,512,512]{2,1,0:T(8,128)(2,1)} %get-tuple-element.158.rows_ref, bf16[8,2,16,512]{3,2,1,0:T(8,128)(2,1)} %copy-done.1, bf16[8,2,16,512]{3,2,1,0:T(8,128)(2,1)} %copy-done.2, ...), custom_call_target="tpu_custom_call", output_to_operand_aliasing={{}: (18, {})} | custom-call | flops 4294967296 | bytes 25165824 | tf_op jit(solution)/shard_map/correlate_other/pallas_call | solution.py:215
  236.2 6.4 %collective-permute-done.23.refs_11_ = bf16[8,2,16,512]{3,2,1,0:T(8,128)(2,1)S(1)} collective-permute-done((bf16[8,2,16,512]{3,2,1,0:T(8,128)(2,1)S(1)}, bf16[8,2,16,512]{3,2,1,0:T(8,128)(2,1)S(1)}, u32[]{:S(2)}, u32[]{:S(2)}) %collective-permute-start.23) | collective-permute-done | bytes 262176 | tf_op jit(solution)/shard_map/ppermute | solution.py:30
  242.7 2.1 collective-permute-start.62
  244.8 11.2 %correlate_own.3 = (f32[16,2,512,1024]{3,2,1,0:T(8,128)}, bf16[8,512,512]{2,1,0:T(8,128)(2,1)}) custom-call(s32[1]{0:T(128)} %bitcast.group_ref, bf16[8,2,16,512]{3,2,1,0:T(8,128)(2,1)} %get-tuple-element.174.refs_0_, bf16[8,2,16,512]{3,2,1,0:T(8,128)(2,1)} %copy-done.8, bf16[8,2,16,512]{3,2,1,0:T(8,128)(2,1)} %copy-done.10, ...), custom_call_target="tpu_custom_call", output_to_operand_aliasing={{0}: (17, {})} | custom-call | flops 4294967296 | bytes 25165824 | tf_op jit(solution)/shard_map/correlate_own/pallas_call | solution.py:215
  257.3 12.5 %correlate_other.3 = f32[16,2,512,1024]{3,2,1,0:T(8,128)} custom-call(s32[1]{0:T(128)} %bitcast.group_ref, bf16[8,512,512]{2,1,0:T(8,128)(2,1)} %get-tuple-element.173.rows_ref, bf16[8,2,16,512]{3,2,1,0:T(8,128)(2,1)} %copy-done.14, bf16[8,2,16,512]{3,2,1,0:T(8,128)(2,1)} %copy-done.20, ...), custom_call_target="tpu_custom_call", output_to_operand_aliasing={{}: (18, {})} | custom-call | flops 4294967296 | bytes 25165824 | tf_op jit(solution)/shard_map/correlate_other/pallas_call | solution.py:215
  (210 shorter events, 38.5 us)
Async XLA Ops:
  1.5 13.9 %collective-permute-start = (bf16[512,1536]{1,0:T(8,128)(2,1)S(1)}, bf16[512,1536]{1,0:T(8,128)(2,1)S(1)}, u32[]{:S(2)}, u32[]{:S(2)}) collective-permute-start(bf16[512,1536]{1,0:T(8,128)(2,1)S(1)} %slice.3), channel_id=1, source_target_pairs={{0,1},{1,2},{2,3},{3,4},{4,5},{5,6},{6,7},{7,8},{8,9},{9,10},{10,1... | collective-permute-start | bytes 4718600 | tf_op jit(solution)/shard_map/ppermute | solution.py:26
  39.0 13.5 %collective-permute-start.24 = (bf16[8,2,16,512]{3,2,1,0:T(8,128)(2,1)}, bf16[8,2,16,512]{3,2,1,0:T(8,128)(2,1)S(1)}, u32[]{:S(2)}, u32[]{:S(2)}) collective-permute-start(bf16[8,2,16,512]{3,2,1,0:T(8,128)(2,1)} %get-tuple-element.147), channel_id=1, source_target_pairs={{0,12},{1,13},{2,14},{3,15},{4,8},{5,9},{6,10},{7,11},{8,4},{9,5},... | collective-permute-start | bytes 786440 | tf_op jit(solution)/shard_map/ppermute | solution.py:30
  44.0 18.0 %collective-permute-start.9 = (bf16[8,2,16,512]{3,2,1,0:T(8,128)(2,1)}, bf16[8,2,16,512]{3,2,1,0:T(8,128)(2,1)S(1)}, u32[]{:S(2)}, u32[]{:S(2)}) collective-permute-start(bf16[8,2,16,512]{3,2,1,0:T(8,128)(2,1)} %get-tuple-element.117), channel_id=1, source_target_pairs={{0,5},{1,4},{2,7},{3,6},{4,1},{5,0},{6,3},{7,2},{8,13},{9,12},{10,... | collective-permute-start | bytes 786440 | tf_op jit(solution)/shard_map/ppermute | solution.py:30
  46.4 22.5 %collective-permute-start.16 = (bf16[8,2,16,512]{3,2,1,0:T(8,128)(2,1)}, bf16[8,2,16,512]{3,2,1,0:T(8,128)(2,1)S(1)}, u32[]{:S(2)}, u32[]{:S(2)}) collective-permute-start(bf16[8,2,16,512]{3,2,1,0:T(8,128)(2,1)} %get-tuple-element.132), channel_id=1, source_target_pairs={{0,8},{1,9},{2,10},{3,11},{4,12},{5,13},{6,14},{7,15},{8,0},{9,1},... | collective-permute-start | bytes 786440 | tf_op jit(solution)/shard_map/ppermute | solution.py:30
  50.6 21.8 %collective-permute-start.33 = (bf16[8,2,16,512]{3,2,1,0:T(8,128)(2,1)S(1)}, bf16[8,2,16,512]{3,2,1,0:T(8,128)(2,1)S(1)}, u32[]{:S(2)}, u32[]{:S(2)}) collective-permute-start(bf16[8,2,16,512]{3,2,1,0:T(8,128)(2,1)S(1)} %collective-permute-done.3.refs_2_), channel_id=1, source_target_pairs={{0,16},{16,0},{1,17},{17,1},{2,18},{18,2},{3,19},{19,3},{4,20},{20... | collective-permute-start | bytes 786440 | tf_op jit(solution)/shard_map/ppermute | solution.py:30
  52.5 19.9 %collective-permute-start.35 = (bf16[8,2,16,512]{3,2,1,0:T(8,128)(2,1)S(1)}, bf16[8,2,16,512]{3,2,1,0:T(8,128)(2,1)S(1)}, u32[]{:S(2)}, u32[]{:S(2)}) collective-permute-start(bf16[8,2,16,512]{3,2,1,0:T(8,128)(2,1)S(1)} %collective-permute-done.8.refs_4_), channel_id=1, source_target_pairs={{0,16},{16,0},{1,17},{17,1},{2,18},{18,2},{3,19},{19,3},{4,20},{20... | collective-permute-start | bytes 786440 | tf_op jit(solution)/shard_map/ppermute | solution.py:30
  54.0 20.0 %collective-permute-start.25 = (bf16[8,2,16,512]{3,2,1,0:T(8,128)(2,1)}, bf16[8,2,16,512]{3,2,1,0:T(8,128)(2,1)S(1)}, u32[]{:S(2)}, u32[]{:S(2)}) collective-permute-start(bf16[8,2,16,512]{3,2,1,0:T(8,128)(2,1)} %get-tuple-element.148), channel_id=1, source_target_pairs={{0,13},{1,12},{2,15},{3,14},{4,9},{5,8},{6,11},{7,10},{8,5},{9,4},... | collective-permute-start | bytes 786440 | tf_op jit(solution)/shard_map/ppermute | solution.py:30
  61.9 12.6 %collective-permute-start.34 = (bf16[8,2,16,512]{3,2,1,0:T(8,128)(2,1)S(1)}, bf16[8,2,16,512]{3,2,1,0:T(8,128)(2,1)S(1)}, u32[]{:S(2)}, u32[]{:S(2)}) collective-permute-start(bf16[8,2,16,512]{3,2,1,0:T(8,128)(2,1)S(1)} %collective-permute-done.4.refs_3_), channel_id=1, source_target_pairs={{0,16},{16,0},{1,17},{17,1},{2,18},{18,2},{3,19},{19,3},{4,20},{20... | collective-permute-start | bytes 786440 | tf_op jit(solution)/shard_map/ppermute | solution.py:30
  68.9 13.7 %collective-permute-start.10 = (bf16[8,2,16,512]{3,2,1,0:T(8,128)(2,1)}, bf16[8,2,16,512]{3,2,1,0:T(8,128)(2,1)S(1)}, u32[]{:S(2)}, u32[]{:S(2)}) collective-permute-start(bf16[8,2,16,512]{3,2,1,0:T(8,128)(2,1)} %get-tuple-element.118), channel_id=1, source_target_pairs={{0,6},{1,7},{2,4},{3,5},{4,2},{5,3},{6,0},{7,1},{8,14},{9,15},{10,... | collective-permute-start | bytes 786440 | tf_op jit(solution)/shard_map/ppermute | solution.py:30
  72.4 20.5 %collective-permute-start.17 = (bf16[8,2,16,512]{3,2,1,0:T(8,128)(2,1)}, bf16[8,2,16,512]{3,2,1,0:T(8,128)(2,1)S(1)}, u32[]{:S(2)}, u32[]{:S(2)}) collective-permute-start(bf16[8,2,16,512]{3,2,1,0:T(8,128)(2,1)} %get-tuple-element.133), channel_id=1, source_target_pairs={{0,9},{1,8},{2,11},{3,10},{4,13},{5,12},{6,15},{7,14},{8,1},{9,0},... | collective-permute-start | bytes 786440 | tf_op jit(solution)/shard_map/ppermute | solution.py:30
  72.4 21.2 %collective-permute-start.43 = (bf16[8,2,16,512]{3,2,1,0:T(8,128)(2,1)S(1)}, bf16[8,2,16,512]{3,2,1,0:T(8,128)(2,1)S(1)}, u32[]{:S(2)}, u32[]{:S(2)}) collective-permute-start(bf16[8,2,16,512]{3,2,1,0:T(8,128)(2,1)S(1)} %collective-permute-done.24.refs_12_), channel_id=1, source_target_pairs={{0,16},{16,0},{1,17},{17,1},{2,18},{18,2},{3,19},{19,3},{4,20},{20... | collective-permute-start | bytes 786440 | tf_op jit(solution)/shard_map/ppermute | solution.py:30
  74.0 19.7 %collective-permute-start.36 = (bf16[8,2,16,512]{3,2,1,0:T(8,128)(2,1)S(1)}, bf16[8,2,16,512]{3,2,1,0:T(8,128)(2,1)S(1)}, u32[]{:S(2)}, u32[]{:S(2)}) collective-permute-start(bf16[8,2,16,512]{3,2,1,0:T(8,128)(2,1)S(1)} %collective-permute-done.9.refs_5_), channel_id=1, source_target_pairs={{0,16},{16,0},{1,17},{17,1},{2,18},{18,2},{3,19},{19,3},{4,20},{20... | collective-permute-start | bytes 786440 | tf_op jit(solution)/shard_map/ppermute | solution.py:30
  74.6 20.7 %collective-permute-start.26 = (bf16[8,2,16,512]{3,2,1,0:T(8,128)(2,1)}, bf16[8,2,16,512]{3,2,1,0:T(8,128)(2,1)S(1)}, u32[]{:S(2)}, u32[]{:S(2)}) collective-permute-start(bf16[8,2,16,512]{3,2,1,0:T(8,128)(2,1)} %get-tuple-element.149), channel_id=1, source_target_pairs={{0,14},{1,15},{2,12},{3,13},{4,10},{5,11},{6,8},{7,9},{8,6},{9,7},... | collective-permute-start | bytes 786440 | tf_op jit(solution)/shard_map/ppermute | solution.py:30
  82.6 13.2 %collective-permute-start.39 = (bf16[8,2,16,512]{3,2,1,0:T(8,128)(2,1)S(1)}, bf16[8,2,16,512]{3,2,1,0:T(8,128)(2,1)S(1)}, u32[]{:S(2)}, u32[]{:S(2)}) collective-permute-start(bf16[8,2,16,512]{3,2,1,0:T(8,128)(2,1)S(1)} %collective-permute-done.16.refs_8_), channel_id=1, source_target_pairs={{0,16},{16,0},{1,17},{17,1},{2,18},{18,2},{3,19},{19,3},{4,20},{20... | collective-permute-start | bytes 786440 | tf_op jit(solution)/shard_map/ppermute | solution.py:30
  95.3 13.3 %collective-permute-start.37 = (bf16[8,2,16,512]{3,2,1,0:T(8,128)(2,1)S(1)}, bf16[8,2,16,512]{3,2,1,0:T(8,128)(2,1)S(1)}, u32[]{:S(2)}, u32[]{:S(2)}) collective-permute-start(bf16[8,2,16,512]{3,2,1,0:T(8,128)(2,1)S(1)} %collective-permute-done.10.refs_6_), channel_id=1, source_target_pairs={{0,16},{16,0},{1,17},{17,1},{2,18},{18,2},{3,19},{19,3},{4,20},{20... | collective-permute-start | bytes 786440 | tf_op jit(solution)/shard_map/ppermute | solution.py:30
  95.9 25.9 %collective-permute-start.18 = (bf16[8,2,16,512]{3,2,1,0:T(8,128)(2,1)S(1)}, bf16[8,2,16,512]{3,2,1,0:T(8,128)(2,1)S(1)}, u32[]{:S(2)}, u32[]{:S(2)}) collective-permute-start(bf16[8,2,16,512]{3,2,1,0:T(8,128)(2,1)S(1)} %copy-done.59), channel_id=1, source_target_pairs={{0,10},{1,11},{2,8},{3,9},{4,14},{5,15},{6,12},{7,13},{8,2},{9,3},... | collective-permute-start | bytes 786440 | tf_op jit(solution)/shard_map/ppermute | solution.py:30
  103.3 18.9 %collective-permute-start.40 = (bf16[8,2,16,512]{3,2,1,0:T(8,128)(2,1)S(1)}, bf16[8,2,16,512]{3,2,1,0:T(8,128)(2,1)S(1)}, u32[]{:S(2)}, u32[]{:S(2)}) collective-permute-start(bf16[8,2,16,512]{3,2,1,0:T(8,128)(2,1)S(1)} %collective-permute-done.17.refs_9_), channel_id=1, source_target_pairs={{0,16},{16,0},{1,17},{17,1},{2,18},{18,2},{3,19},{19,3},{4,20},{20... | collective-permute-start | bytes 786440 | tf_op jit(solution)/shard_map/ppermute | solution.py:30
  103.9 18.5 %collective-permute-start.27 = (bf16[8,2,16,512]{3,2,1,0:T(8,128)(2,1)S(1)}, bf16[8,2,16,512]{3,2,1,0:T(8,128)(2,1)S(1)}, u32[]{:S(2)}, u32[]{:S(2)}) collective-permute-start(bf16[8,2,16,512]{3,2,1,0:T(8,128)(2,1)S(1)} %copy-done.58), channel_id=1, source_target_pairs={{0,15},{1,14},{2,13},{3,12},{4,11},{5,10},{6,9},{7,8},{8,7},{9,6},... | collective-permute-start | bytes 786440 | tf_op jit(solution)/shard_map/ppermute | solution.py:30
  105.4 18.5 %collective-permute-start.6 = (bf16[8,2,16,512]{3,2,1,0:T(8,128)(2,1)}, bf16[8,2,16,512]{3,2,1,0:T(8,128)(2,1)S(1)}, u32[]{:S(2)}, u32[]{:S(2)}) collective-permute-start(bf16[8,2,16,512]{3,2,1,0:T(8,128)(2,1)} %get-tuple-element.109), channel_id=1, source_target_pairs={{0,2},{1,3},{2,0},{3,1},{4,6},{5,7},{6,4},{7,5},{8,10},{9,11},{10,... | collective-permute-start | bytes 786440 | tf_op jit(solution)/shard_map/ppermute | solution.py:30
  108.5 24.7 %collective-permute-start.45 = (bf16[8,2,16,512]{3,2,1,0:T(8,128)(2,1)S(1)}, bf16[8,2,16,512]{3,2,1,0:T(8,128)(2,1)S(1)}, u32[]{:S(2)}, u32[]{:S(2)}) collective-permute-start(bf16[8,2,16,512]{3,2,1,0:T(8,128)(2,1)S(1)} %collective-permute-done.26.refs_14_), channel_id=1, source_target_pairs={{0,16},{16,0},{1,17},{17,1},{2,18},{18,2},{3,19},{19,3},{4,20},{20... | collective-permute-start | bytes 786440 | tf_op jit(solution)/shard_map/ppermute | solution.py:30
  122.3 16.1 %collective-permute-start.19 = (bf16[8,2,16,512]{3,2,1,0:T(8,128)(2,1)S(1)}, bf16[8,2,16,512]{3,2,1,0:T(8,128)(2,1)S(1)}, u32[]{:S(2)}, u32[]{:S(2)}) collective-permute-start(bf16[8,2,16,512]{3,2,1,0:T(8,128)(2,1)S(1)} %copy-done.55), channel_id=1, source_target_pairs={{0,11},{1,10},{2,9},{3,8},{4,15},{5,14},{6,13},{7,12},{8,3},{9,2},... | collective-permute-start | bytes 786440 | tf_op jit(solution)/shard_map/ppermute | solution.py:30
  122.4 16.9 %collective-permute-start.41 = (bf16[8,2,16,512]{3,2,1,0:T(8,128)(2,1)S(1)}, bf16[8,2,16,512]{3,2,1,0:T(8,128)(2,1)S(1)}, u32[]{:S(2)}, u32[]{:S(2)}) collective-permute-start(bf16[8,2,16,512]{3,2,1,0:T(8,128)(2,1)S(1)} %collective-permute-done.18.refs_10_), channel_id=1, source_target_pairs={{0,16},{16,0},{1,17},{17,1},{2,18},{18,2},{3,19},{19,3},{4,20},{20... | collective-permute-start | bytes 786440 | tf_op jit(solution)/shard_map/ppermute | solution.py:30
  123.9 20.0 %collective-permute-start.12 = (bf16[8,2,16,512]{3,2,1,0:T(8,128)(2,1)}, bf16[8,2,16,512]{3,2,1,0:T(8,128)(2,1)S(1)}, u32[]{:S(2)}, u32[]{:S(2)}) collective-permute-start(bf16[8,2,16,512]{3,2,1,0:T(8,128)(2,1)} %get-tuple-element.120), channel_id=1, source_target_pairs={{0,4},{1,5},{2,6},{3,7},{4,0},{5,1},{6,2},{7,3},{8,12},{9,13},{10,... | collective-permute-start | bytes 786440 | tf_op jit(solution)/shard_map/ppermute | solution.py:30
  139.3 15.4 %collective-permute-start.42 = (bf16[8,2,16,512]{3,2,1,0:T(8,128)(2,1)S(1)}, bf16[8,2,16,512]{3,2,1,0:T(8,128)(2,1)}, u32[]{:S(2)}, u32[]{:S(2)}) collective-permute-start(bf16[8,2,16,512]{3,2,1,0:T(8,128)(2,1)S(1)} %collective-permute-done.19.refs_11_), channel_id=1, source_target_pairs={{0,16},{16,0},{1,17},{17,1},{2,18},{18,2},{3,19},{19,3},{4,20},{20... | collective-permute-start | bytes 786440 | tf_op jit(solution)/shard_map/ppermute | solution.py:30
  144.9 17.1 %collective-permute-start.13 = (bf16[8,2,16,512]{3,2,1,0:T(8,128)(2,1)}, bf16[8,2,16,512]{3,2,1,0:T(8,128)(2,1)S(1)}, u32[]{:S(2)}, u32[]{:S(2)}) collective-permute-start(bf16[8,2,16,512]{3,2,1,0:T(8,128)(2,1)} %get-tuple-element.122), channel_id=1, source_target_pairs={{0,5},{1,4},{2,7},{3,6},{4,1},{5,0},{6,3},{7,2},{8,13},{9,12},{10,... | collective-permute-start | bytes 786440 | tf_op jit(solution)/shard_map/ppermute | solution.py:30
  145.0 30.0 %collective-permute-start.20 = (bf16[8,2,16,512]{3,2,1,0:T(8,128)(2,1)}, bf16[8,2,16,512]{3,2,1,0:T(8,128)(2,1)}, u32[]{:S(2)}, u32[]{:S(2)}) collective-permute-start(bf16[8,2,16,512]{3,2,1,0:T(8,128)(2,1)} %get-tuple-element.136), channel_id=1, source_target_pairs={{0,8},{1,9},{2,10},{3,11},{4,12},{5,13},{6,14},{7,15},{8,0},{9,1},... | collective-permute-start | bytes 786440 | tf_op jit(solution)/shard_map/ppermute | solution.py:30
  149.0 26.1 %collective-permute-start.48 = (bf16[8,2,16,512]{3,2,1,0:T(8,128)(2,1)S(1)}, bf16[8,2,16,512]{3,2,1,0:T(8,128)(2,1)S(1)}, u32[]{:S(2)}, u32[]{:S(2)}) collective-permute-start(bf16[8,2,16,512]{3,2,1,0:T(8,128)(2,1)S(1)} %collective-permute-done.5.refs_1_), channel_id=1, source_target_pairs={{0,16},{16,0},{1,17},{17,1},{2,18},{18,2},{3,19},{19,3},{4,20},{20... | collective-permute-start | bytes 786440 | tf_op jit(solution)/shard_map/ppermute | solution.py:30
  154.7 20.5 %collective-permute-start.50 = (bf16[8,2,16,512]{3,2,1,0:T(8,128)(2,1)S(1)}, bf16[8,2,16,512]{3,2,1,0:T(8,128)(2,1)S(1)}, u32[]{:S(2)}, u32[]{:S(2)}) collective-permute-start(bf16[8,2,16,512]{3,2,1,0:T(8,128)(2,1)S(1)} %collective-permute-done.7.refs_3_), channel_id=1, source_target_pairs={{0,16},{16,0},{1,17},{17,1},{2,18},{18,2},{3,19},{19,3},{4,20},{20... | collective-permute-start | bytes 786440 | tf_op jit(solution)/shard_map/ppermute | solution.py:30
  156.4 20.3 %collective-permute-start.49 = (bf16[8,2,16,512]{3,2,1,0:T(8,128)(2,1)S(1)}, bf16[8,2,16,512]{3,2,1,0:T(8,128)(2,1)S(1)}, u32[]{:S(2)}, u32[]{:S(2)}) collective-permute-start(bf16[8,2,16,512]{3,2,1,0:T(8,128)(2,1)S(1)} %collective-permute-done.6.refs_2_), channel_id=1, source_target_pairs={{0,16},{16,0},{1,17},{17,1},{2,18},{18,2},{3,19},{19,3},{4,20},{20... | collective-permute-start | bytes 786440 | tf_op jit(solution)/shard_map/ppermute | solution.py:30
  162.1 15.3 %collective-permute-start.29 = (bf16[8,2,16,512]{3,2,1,0:T(8,128)(2,1)}, bf16[8,2,16,512]{3,2,1,0:T(8,128)(2,1)S(1)}, u32[]{:S(2)}, u32[]{:S(2)}) collective-permute-start(bf16[8,2,16,512]{3,2,1,0:T(8,128)(2,1)} %get-tuple-element.153), channel_id=1, source_target_pairs={{0,13},{1,12},{2,15},{3,14},{4,9},{5,8},{6,11},{7,10},{8,5},{9,4},... | collective-permute-start | bytes 786440 | tf_op jit(solution)/shard_map/ppermute | solution.py:30
  175.1 21.2 %collective-permute-start.21 = (bf16[8,2,16,512]{3,2,1,0:T(8,128)(2,1)}, bf16[8,2,16,512]{3,2,1,0:T(8,128)(2,1)}, u32[]{:S(2)}, u32[]{:S(2)}) collective-permute-start(bf16[8,2,16,512]{3,2,1,0:T(8,128)(2,1)} %get-tuple-element.138), channel_id=1, source_target_pairs={{0,9},{1,8},{2,11},{3,10},{4,13},{5,12},{6,15},{7,14},{8,1},{9,0},... | collective-permute-start | bytes 786440 | tf_op jit(solution)/shard_map/ppermute | solution.py:30
  175.2 21.1 %collective-permute-start.51 = (bf16[8,2,16,512]{3,2,1,0:T(8,128)(2,1)S(1)}, bf16[8,2,16,512]{3,2,1,0:T(8,128)(2,1)}, u32[]{:S(2)}, u32[]{:S(2)}) collective-permute-start(bf16[8,2,16,512]{3,2,1,0:T(8,128)(2,1)S(1)} %collective-permute-done.12.refs_4_), channel_id=1, source_target_pairs={{0,16},{16,0},{1,17},{17,1},{2,18},{18,2},{3,19},{19,3},{4,20},{20... | collective-permute-start | bytes 786440 | tf_op jit(solution)/shard_map/ppermute | solution.py:30
  176.7 22.7 %collective-permute-start.55 = (bf16[8,2,16,512]{3,2,1,0:T(8,128)(2,1)}, bf16[8,2,16,512]{3,2,1,0:T(8,128)(2,1)}, u32[]{:S(2)}, u32[]{:S(2)}) collective-permute-start(bf16[8,2,16,512]{3,2,1,0:T(8,128)(2,1)} %collective-permute-done.20.refs_8_), channel_id=1, source_target_pairs={{0,16},{16,0},{1,17},{17,1},{2,18},{18,2},{3,19},{19,3},{4,20},{20... | collective-permute-start | bytes 786440 | tf_op jit(solution)/shard_map/ppermute | solution.py:30
  177.4 23.7 %collective-permute-start.59 = (bf16[8,2,16,512]{3,2,1,0:T(8,128)(2,1)}, bf16[8,2,16,512]{3,2,1,0:T(8,128)(2,1)}, u32[]{:S(2)}, u32[]{:S(2)}) collective-permute-start(bf16[8,2,16,512]{3,2,1,0:T(8,128)(2,1)} %collective-permute-done.28.refs_12_), channel_id=1, source_target_pairs={{0,16},{16,0},{1,17},{17,1},{2,18},{18,2},{3,19},{19,3},{4,20},{20... | collective-permute-start | bytes 786440 | tf_op jit(solution)/shard_map/ppermute | solution.py:30
  185.4 16.0 %collective-permute-start.30 = (bf16[8,2,16,512]{3,2,1,0:T(8,128)(2,1)}, bf16[8,2,16,512]{3,2,1,0:T(8,128)(2,1)}, u32[]{:S(2)}, u32[]{:S(2)}) collective-permute-start(bf16[8,2,16,512]{3,2,1,0:T(8,128)(2,1)} %get-tuple-element.155), channel_id=1, source_target_pairs={{0,14},{1,15},{2,12},{3,13},{4,10},{5,11},{6,8},{7,9},{8,6},{9,7},... | collective-permute-start | bytes 786440 | tf_op jit(solution)/shard_map/ppermute | solution.py:30
  196.3 25.1 %collective-permute-start.15 = (bf16[8,2,16,512]{3,2,1,0:T(8,128)(2,1)}, bf16[8,2,16,512]{3,2,1,0:T(8,128)(2,1)S(1)}, u32[]{:S(2)}, u32[]{:S(2)}) collective-permute-start(bf16[8,2,16,512]{3,2,1,0:T(8,128)(2,1)} %get-tuple-element.126), channel_id=1, source_target_pairs={{0,7},{1,6},{2,5},{3,4},{4,3},{5,2},{6,1},{7,0},{8,15},{9,14},{10,... | collective-permute-start | bytes 786440 | tf_op jit(solution)/shard_map/ppermute | solution.py:30
  196.3 18.6 %collective-permute-start.22 = (bf16[8,2,16,512]{3,2,1,0:T(8,128)(2,1)}, bf16[8,2,16,512]{3,2,1,0:T(8,128)(2,1)S(1)}, u32[]{:S(2)}, u32[]{:S(2)}) collective-permute-start(bf16[8,2,16,512]{3,2,1,0:T(8,128)(2,1)} %get-tuple-element.140), channel_id=1, source_target_pairs={{0,10},{1,11},{2,8},{3,9},{4,14},{5,15},{6,12},{7,13},{8,2},{9,3},... | collective-permute-start | bytes 786440 | tf_op jit(solution)/shard_map/ppermute | solution.py:30
  199.4 15.8 %collective-permute-start.52 = (bf16[8,2,16,512]{3,2,1,0:T(8,128)(2,1)}, bf16[8,2,16,512]{3,2,1,0:T(8,128)(2,1)S(1)}, u32[]{:S(2)}, u32[]{:S(2)}) collective-permute-start(bf16[8,2,16,512]{3,2,1,0:T(8,128)(2,1)} %copy-done.22), channel_id=1, source_target_pairs={{0,16},{16,0},{1,17},{17,1},{2,18},{18,2},{3,19},{19,3},{4,20},{20... | collective-permute-start | bytes 786440 | tf_op jit(solution)/shard_map/ppermute | solution.py:30
  201.0 18.2 %collective-permute-start.56 = (bf16[8,2,16,512]{3,2,1,0:T(8,128)(2,1)}, bf16[8,2,16,512]{3,2,1,0:T(8,128)(2,1)S(1)}, u32[]{:S(2)}, u32[]{:S(2)}) collective-permute-start(bf16[8,2,16,512]{3,2,1,0:T(8,128)(2,1)} %collective-permute-done.21.refs_9_), channel_id=1, source_target_pairs={{0,16},{16,0},{1,17},{17,1},{2,18},{18,2},{3,19},{19,3},{4,20},{20... | collective-permute-start | bytes 786440 | tf_op jit(solution)/shard_map/ppermute | solution.py:30
  201.4 19.9 %collective-permute-start.60 = (bf16[8,2,16,512]{3,2,1,0:T(8,128)(2,1)}, bf16[8,2,16,512]{3,2,1,0:T(8,128)(2,1)S(1)}, u32[]{:S(2)}, u32[]{:S(2)}) collective-permute-start(bf16[8,2,16,512]{3,2,1,0:T(8,128)(2,1)} %copy-done.25), channel_id=1, source_target_pairs={{0,16},{16,0},{1,17},{17,1},{2,18},{18,2},{3,19},{19,3},{4,20},{20... | collective-permute-start | bytes 786440 | tf_op jit(solution)/shard_map/ppermute | solution.py:30
  214.9 27.8 %collective-permute-start.31 = (bf16[8,2,16,512]{3,2,1,0:T(8,128)(2,1)S(1)}, bf16[8,2,16,512]{3,2,1,0:T(8,128)(2,1)S(1)}, u32[]{:S(2)}, u32[]{:S(2)}) collective-permute-start(bf16[8,2,16,512]{3,2,1,0:T(8,128)(2,1)S(1)} %copy-done.48), channel_id=1, source_target_pairs={{0,15},{1,14},{2,13},{3,12},{4,11},{5,10},{6,9},{7,8},{8,7},{9,6},... | collective-permute-start | bytes 786440 | tf_op jit(solution)/shard_map/ppermute | solution.py:30
  215.2 27.4 %collective-permute-start.23 = (bf16[8,2,16,512]{3,2,1,0:T(8,128)(2,1)S(1)}, bf16[8,2,16,512]{3,2,1,0:T(8,128)(2,1)S(1)}, u32[]{:S(2)}, u32[]{:S(2)}) collective-permute-start(bf16[8,2,16,512]{3,2,1,0:T(8,128)(2,1)S(1)} %copy-done.49), channel_id=1, source_target_pairs={{0,11},{1,10},{2,9},{3,8},{4,15},{5,14},{6,13},{7,12},{8,3},{9,2},... | collective-permute-start | bytes 786440 | tf_op jit(solution)/shard_map/ppermute | solution.py:30
  219.2 16.8 %collective-permute-start.53 = (bf16[8,2,16,512]{3,2,1,0:T(8,128)(2,1)S(1)}, bf16[8,2,16,512]{3,2,1,0:T(8,128)(2,1)S(1)}, u32[]{:S(2)}, u32[]{:S(2)}) collective-permute-start(bf16[8,2,16,512]{3,2,1,0:T(8,128)(2,1)S(1)} %copy-done.27), channel_id=1, source_target_pairs={{0,16},{16,0},{1,17},{17,1},{2,18},{18,2},{3,19},{19,3},{4,20},{20... | collective-permute-start | bytes 786440 | tf_op jit(solution)/shard_map/ppermute | solution.py:30
  221.3 21.3 %collective-permute-start.57 = (bf16[8,2,16,512]{3,2,1,0:T(8,128)(2,1)S(1)}, bf16[8,2,16,512]{3,2,1,0:T(8,128)(2,1)S(1)}, u32[]{:S(2)}, u32[]{:S(2)}) collective-permute-start(bf16[8,2,16,512]{3,2,1,0:T(8,128)(2,1)S(1)} %collective-permute-done.22.refs_10_), channel_id=1, source_target_pairs={{0,16},{16,0},{1,17},{17,1},{2,18},{18,2},{3,19},{19,3},{4,20},{20... | collective-permute-start | bytes 786440 | tf_op jit(solution)/shard_map/ppermute | solution.py:30
  221.4 21.3 %collective-permute-start.61 = (bf16[8,2,16,512]{3,2,1,0:T(8,128)(2,1)}, bf16[8,2,16,512]{3,2,1,0:T(8,128)(2,1)S(1)}, u32[]{:S(2)}, u32[]{:S(2)}) collective-permute-start(bf16[8,2,16,512]{3,2,1,0:T(8,128)(2,1)} %collective-permute-done.30.refs_14_), channel_id=1, source_target_pairs={{0,16},{16,0},{1,17},{17,1},{2,18},{18,2},{3,19},{19,3},{4,20},{20... | collective-permute-start | bytes 786440 | tf_op jit(solution)/shard_map/ppermute | solution.py:30
  236.1 20.0 %collective-permute-start.54 = (bf16[8,2,16,512]{3,2,1,0:T(8,128)(2,1)S(1)}, bf16[8,2,16,512]{3,2,1,0:T(8,128)(2,1)S(1)}, u32[]{:S(2)}, u32[]{:S(2)}) collective-permute-start(bf16[8,2,16,512]{3,2,1,0:T(8,128)(2,1)S(1)} %collective-permute-done.15.refs_7_), channel_id=1, source_target_pairs={{0,16},{16,0},{1,17},{17,1},{2,18},{18,2},{3,19},{19,3},{4,20},{20... | collective-permute-start | bytes 786440 | tf_op jit(solution)/shard_map/ppermute | solution.py:30
  242.6 13.5 %collective-permute-start.58 = (bf16[8,2,16,512]{3,2,1,0:T(8,128)(2,1)S(1)}, bf16[8,2,16,512]{3,2,1,0:T(8,128)(2,1)S(1)}, u32[]{:S(2)}, u32[]{:S(2)}) collective-permute-start(bf16[8,2,16,512]{3,2,1,0:T(8,128)(2,1)S(1)} %collective-permute-done.23.refs_11_), channel_id=1, source_target_pairs={{0,16},{16,0},{1,17},{17,1},{2,18},{18,2},{3,19},{19,3},{4,20},{20... | collective-permute-start | bytes 786440 | tf_op jit(solution)/shard_map/ppermute | solution.py:30
  242.7 13.9 %collective-permute-start.62 = (bf16[8,2,16,512]{3,2,1,0:T(8,128)(2,1)S(1)}, bf16[8,2,16,512]{3,2,1,0:T(8,128)(2,1)S(1)}, u32[]{:S(2)}, u32[]{:S(2)}) collective-permute-start(bf16[8,2,16,512]{3,2,1,0:T(8,128)(2,1)S(1)} %collective-permute-done.31.refs_15_), channel_id=1, source_target_pairs={{0,16},{16,0},{1,17},{17,1},{2,18},{18,2},{3,19},{19,3},{4,20},{20... | collective-permute-start | bytes 786440 | tf_op jit(solution)/shard_map/ppermute | solution.py:30
  (77 other events, 2693.9 us)
